TPU v7x, 32 devices: a whole 2x2x4 slice. The times are simulated.
32 devices in a mesh: dp: 8 (over z, y), mp: 4 (over x, core).
Axes of the slice: x: 2, y: 2, z: 4, core: 2. Of those that a mesh axis runs over, the one named last changes fastest.
Arguments:
- patches: bfloat16 [64, 196, 1024], P('dp'), may hold values from -6 to 6
- keep_mask: int32 [64, 196], P('dp'), may hold values from 0 to 1, as said below
- w_query: bfloat16 [1024, 1024], P(None, 'mp'), may hold values from -0.1875 to 0.1875
- w_key: bfloat16 [1024, 1024], P(None, 'mp'), may hold values from -0.1875 to 0.1875
- w_value: bfloat16 [1024, 1024], P(None, 'mp'), may hold values from -0.1875 to 0.1875
- w_out: bfloat16 [1024, 1024], P('mp'), may hold values from -0.5 to 0.5
- w_up: bfloat16 [1024, 4096], P(None, 'mp'), may hold values from -0.1875 to 0.1875
- w_down: bfloat16 [4096, 1024], P('mp'), may hold values from -0.09375 to 0.09375
- gain_attn: float32 [1024], replicated, may hold values from 0.5 to 1.5
- gain_mlp: float32 [1024], replicated, may hold values from 0.5 to 1.5
- gain_learn: float32 [1024], replicated, may hold values from 0.5 to 1.5
- w_learn: bfloat16 [1024, 64], P('dp'), may hold values from -0.1875 to 0.1875
- w_select: bfloat16 [64, 8], replicated, may hold values from -0.75 to 0.75
- cotangent: bfloat16 [64, 8, 1024], P('dp'), may hold values from -96 to 96
Outputs:
- learned: bfloat16 [64, 8, 1024], P('dp')
- block_out: bfloat16 [64, 196, 1024], P('dp')
- grad_patches: bfloat16 [64, 196, 1024], P('dp')
- grad_query: float32 [1024, 1024], P(None, 'mp')
- grad_key: float32 [1024, 1024], P(None, 'mp')
- grad_value: float32 [1024, 1024], P(None, 'mp')
- grad_out: float32 [1024, 1024], P('mp')
- grad_up: float32 [1024, 4096], P(None, 'mp')
- grad_down: float32 [4096, 1024], P('mp')
- grad_gain_attn: float32 [1024], replicated
- grad_gain_mlp: float32 [1024], replicated
- grad_gain_learn: float32 [1024], replicated
- grad_learn: float32 [1024, 64], P('dp')
- grad_select: float32 [64, 8], replicated
Inputs may be any that keep to these rules, and one draw needn't show every extreme that they name: `keep_mask`: every image keeps at least one patch.
All inputs are finite; a program needn't handle non-finite values.
Results may differ from a plain program's by a relative error of at most 0.025.
Values may be sent and summed in bfloat16 or wider, within the bound.
A program may use at most 192 MiB of HBM per device.

v0:
```python
import math

import jax
import jax.numpy as jnp
from jax import lax
from jax.sharding import PartitionSpec as P

D = 1024
HEADS = 16


def product(left, right):
    return jnp.dot(left, right, preferred_element_type=jnp.float32)


def contract_rows(left, right):
    return lax.dot_general(
        left, right, (((0,), (0,)), ((), ())), preferred_element_type=jnp.float32
    )


def contract_cols(left, right):
    return lax.dot_general(
        left, right, (((1,), (1,)), ((), ())), preferred_element_type=jnp.float32
    )


def normalize(inputs):
    row_mean = jnp.mean(inputs, axis=-1, keepdims=True)
    centered = inputs - row_mean
    inverse = lax.rsqrt(jnp.mean(centered * centered, axis=-1, keepdims=True) + 1e-06)
    return (centered * inverse, inverse)


def norm_back(grad_norm, normed, inverse, gain):
    scaled_grad = grad_norm * gain
    grad_input = inverse * (
        scaled_grad
        - jnp.mean(scaled_grad, axis=-1, keepdims=True)
        - normed * jnp.mean(scaled_grad * normed, axis=-1, keepdims=True)
    )
    return (grad_input, jnp.sum(grad_norm * normed, axis=0))


def gelu_exact(inputs):
    return jax.nn.gelu(inputs, approximate=False)


def gelu_back(hidden_pre, grad_act):
    _, pullback = jax.vjp(gelu_exact, hidden_pre)
    return pullback(grad_act)[0]


def local(
    patches,
    keep_mask,
    w_query,
    w_key,
    w_value,
    w_out,
    w_up,
    w_down,
    gain_attn,
    gain_mlp,
    gain_learn,
    w_learn,
    w_select,
    cotangent,
):
    images, patch_count, feature_count = patches.shape
    row_count = images * patch_count
    head_size = D // HEADS
    heads_here = w_query.shape[1] // head_size
    score_scale = 1.0 / math.sqrt(head_size)
    visible = keep_mask > 0
    head_shape = (images, patch_count, heads_here, head_size)
    residual_rows = patches.reshape(row_count, feature_count).astype(jnp.float32)
    normed_one, inverse_one = normalize(residual_rows)
    attn_input = (normed_one * gain_attn).astype(jnp.bfloat16)
    query_flat = product(attn_input, w_query).astype(jnp.bfloat16)
    key_flat = product(attn_input, w_key).astype(jnp.bfloat16)
    value_flat = product(attn_input, w_value).astype(jnp.bfloat16)
    query_heads = query_flat.reshape(head_shape)
    key_heads = key_flat.reshape(head_shape)
    value_heads = value_flat.reshape(head_shape)

    def masked_scores():
        raw_scores = (
            jnp.einsum(
                "bqhe,bkhe->bhqk", query_heads, key_heads, preferred_element_type=jnp.float32
            )
            * score_scale
        )
        return jnp.where(visible[:, None, None, :], raw_scores, -1e30)

    scores = masked_scores()
    top_score = jnp.max(scores, axis=-1, keepdims=True)
    exponent = jnp.exp(scores - top_score)
    denominator = jnp.sum(exponent, axis=-1, keepdims=True)
    logsum = top_score + jnp.log(denominator)
    probs_low = (exponent / denominator).astype(jnp.bfloat16)
    mixed_heads = jnp.einsum(
        "bhqk,bkhe->bqhe", probs_low, value_heads, preferred_element_type=jnp.float32
    )
    mixed_heads = mixed_heads.astype(jnp.bfloat16).reshape(row_count, heads_here * head_size)
    attn_term = product(mixed_heads, w_out)
    hidden_one = residual_rows + lax.psum(attn_term.astype(jnp.bfloat16), "mp").astype(jnp.float32)
    normed_two, inverse_two = normalize(hidden_one)
    mlp_input = (normed_two * gain_mlp).astype(jnp.bfloat16)
    hidden_pre = product(mlp_input, w_up)
    activated = gelu_exact(hidden_pre).astype(jnp.bfloat16)
    mlp_out = lax.psum(product(activated, w_down).astype(jnp.bfloat16), "mp").astype(jnp.float32)
    block_rows = (hidden_one + mlp_out).astype(jnp.bfloat16)
    normed_learn, inverse_learn = normalize(block_rows.astype(jnp.float32))
    learn_input = (normed_learn * gain_learn).astype(jnp.bfloat16)
    learn_full = lax.all_gather(w_learn, "dp", axis=0, tiled=True)
    learn_pre = product(learn_input, learn_full)
    learn_act = gelu_exact(learn_pre).astype(jnp.bfloat16)
    logits = product(learn_act, w_select).reshape(images, patch_count, -1)
    logits = jnp.where(visible[:, :, None], logits, -1e30)
    top_logit = jnp.max(logits, axis=1, keepdims=True)
    exp_logit = jnp.exp(logits - top_logit)
    token_maps = exp_logit / jnp.sum(exp_logit, axis=1, keepdims=True)
    maps_low = token_maps.astype(jnp.bfloat16)
    block_three = block_rows.reshape(images, patch_count, feature_count)
    learned = jnp.einsum(
        "bpn,bpd->bnd", maps_low, block_three, preferred_element_type=jnp.float32
    ).astype(jnp.bfloat16)
    grad_maps = jnp.einsum(
        "bnd,bpd->bpn", cotangent, block_three, preferred_element_type=jnp.float32
    )
    grad_block = jnp.einsum(
        "bpn,bnd->bpd", maps_low, cotangent, preferred_element_type=jnp.float32
    ).reshape(row_count, feature_count)
    grad_logits = token_maps * (grad_maps - jnp.sum(token_maps * grad_maps, axis=1, keepdims=True))
    grad_logits = grad_logits.reshape(row_count, -1).astype(jnp.bfloat16)
    grad_select = contract_rows(learn_act, grad_logits)
    grad_learn_act = contract_cols(grad_logits, w_select)
    grad_learn_pre = gelu_back(learn_pre, grad_learn_act).astype(jnp.bfloat16)
    grad_learn = contract_rows(learn_input, grad_learn_pre)
    grad_learn_input = contract_cols(grad_learn_pre, learn_full)
    grad_from_learn, grad_gain_learn = norm_back(
        grad_learn_input, normed_learn, inverse_learn, gain_learn
    )
    grad_hidden = grad_block + grad_from_learn
    grad_hidden_low = grad_hidden.astype(jnp.bfloat16)
    grad_down = contract_rows(activated, grad_hidden_low)
    grad_act = contract_cols(grad_hidden_low, w_down)
    grad_pre = gelu_back(hidden_pre, grad_act).astype(jnp.bfloat16)
    grad_up = contract_rows(mlp_input, grad_pre)
    mlp_back_term = contract_cols(grad_pre, w_up)
    grad_mlp_input = lax.psum(mlp_back_term.astype(jnp.bfloat16), "mp").astype(jnp.float32)
    grad_from_two, grad_gain_mlp = norm_back(grad_mlp_input, normed_two, inverse_two, gain_mlp)
    grad_hidden = grad_hidden + grad_from_two
    grad_attn_low = grad_hidden.astype(jnp.bfloat16)
    grad_out = contract_rows(mixed_heads, grad_attn_low)
    grad_mixed = contract_cols(grad_attn_low, w_out).astype(jnp.bfloat16).reshape(head_shape)
    probs_again = jnp.exp(masked_scores() - logsum)
    probs_again_low = probs_again.astype(jnp.bfloat16)
    grad_probs = jnp.einsum(
        "bqhe,bkhe->bhqk", grad_mixed, value_heads, preferred_element_type=jnp.float32
    )
    grad_value_heads = jnp.einsum(
        "bhqk,bqhe->bkhe", probs_again_low, grad_mixed, preferred_element_type=jnp.float32
    ).astype(jnp.bfloat16)
    grad_scores = probs_again * (
        grad_probs - jnp.sum(probs_again * grad_probs, axis=-1, keepdims=True)
    )
    grad_scores = grad_scores.astype(jnp.bfloat16)
    grad_query_heads = (
        jnp.einsum("bhqk,bkhe->bqhe", grad_scores, key_heads, preferred_element_type=jnp.float32)
        * score_scale
    ).astype(jnp.bfloat16)
    grad_key_heads = (
        jnp.einsum("bhqk,bqhe->bkhe", grad_scores, query_heads, preferred_element_type=jnp.float32)
        * score_scale
    ).astype(jnp.bfloat16)
    grad_query_flat = grad_query_heads.reshape(row_count, -1)
    grad_key_flat = grad_key_heads.reshape(row_count, -1)
    grad_value_flat = grad_value_heads.reshape(row_count, -1)
    grad_query = contract_rows(attn_input, grad_query_flat)
    grad_key = contract_rows(attn_input, grad_key_flat)
    grad_value = contract_rows(attn_input, grad_value_flat)
    attn_terms = (
        contract_cols(grad_query_flat, w_query)
        + contract_cols(grad_key_flat, w_key)
        + contract_cols(grad_value_flat, w_value)
    )
    grad_attn_input = lax.psum(attn_terms.astype(jnp.bfloat16), "mp").astype(jnp.float32)
    grad_from_one, grad_gain_attn = norm_back(grad_attn_input, normed_one, inverse_one, gain_attn)
    grad_patches = (
        (grad_hidden + grad_from_one)
        .astype(jnp.bfloat16)
        .reshape(images, patch_count, feature_count)
    )
    (
        grad_query,
        grad_key,
        grad_value,
        grad_out,
        grad_gain_attn,
        grad_up,
        grad_down,
        grad_gain_mlp,
        grad_gain_learn,
        grad_select,
        grad_learn,
    ) = (
        lax.psum(grad_query.astype(jnp.bfloat16), "dp").astype(jnp.float32),
        lax.psum(grad_key.astype(jnp.bfloat16), "dp").astype(jnp.float32),
        lax.psum(grad_value.astype(jnp.bfloat16), "dp").astype(jnp.float32),
        lax.psum(grad_out.astype(jnp.bfloat16), "dp").astype(jnp.float32),
        lax.psum(grad_gain_attn.astype(jnp.bfloat16), "dp").astype(jnp.float32),
        lax.psum(grad_up.astype(jnp.bfloat16), "dp").astype(jnp.float32),
        lax.psum(grad_down.astype(jnp.bfloat16), "dp").astype(jnp.float32),
        lax.psum(grad_gain_mlp.astype(jnp.bfloat16), "dp").astype(jnp.float32),
        lax.psum(grad_gain_learn.astype(jnp.bfloat16), "dp").astype(jnp.float32),
        lax.psum(grad_select.astype(jnp.bfloat16), "dp").astype(jnp.float32),
        lax.psum(grad_learn.astype(jnp.bfloat16), "dp").astype(jnp.float32),
    )
    learn_rows = w_learn.shape[0]
    grad_learn = lax.dynamic_slice_in_dim(
        grad_learn, lax.axis_index("dp") * learn_rows, learn_rows, 0
    )
    return (
        learned,
        block_three,
        grad_patches,
        grad_query,
        grad_key,
        grad_value,
        grad_out,
        grad_up,
        grad_down,
        grad_gain_attn,
        grad_gain_mlp,
        grad_gain_learn,
        grad_learn,
        grad_select,
    )


def solution(mesh):
    return jax.shard_map(
        local,
        mesh=mesh,
        in_specs=(
            P("dp", None, None),
            P("dp", None),
            P(None, "mp"),
            P(None, "mp"),
            P(None, "mp"),
            P("mp", None),
            P(None, "mp"),
            P("mp", None),
            P(),
            P(),
            P(),
            P("dp", None),
            P(),
            P("dp", None, None),
        ),
        out_specs=(
            P("dp", None, None),
            P("dp", None, None),
            P("dp", None, None),
            P(None, "mp"),
            P(None, "mp"),
            P(None, "mp"),
            P("mp", None),
            P(None, "mp"),
            P("mp", None),
            P(),
            P(),
            P(),
            P("dp", None),
            P(),
        ),
        check_vma=False,
    )
```

profile of v0, /device:TPU:0, one launch (start us, length us, event | category | flops | bytes accessed | tf_op | source)
XLA Modules:
  0.0 764.7 jit_solution(10205588841361691865)
XLA Ops:
  7.3 6.7 copy.100
  14.7 6.3 reshape.225
  68.9 72.3 %all-reduce.8.cloned.1.call-done = bf16[1568,1024]{1,0:T(8,128)(2,1)} async-done(((bf16[1568,1024]{1,0:T(8,128)(2,1)}), bf16[1568,1024]{1,0:T(8,128)(2,1)}) %all-reduce.8.cloned.1.call-update) | async-done | bytes 3211280 | tf_op jit(solution)/shard_map/psum | solution.py:107
  146.6 19.8 %multiply_convert_fusion.2 = (bf16[1568,1024]{1,0:T(8,128)(2,1)S(1)}, f32[1568,1024]{1,0:T(8,128)}, f32[1568,1024]{1,0:T(8,128)}) fusion(bf16[1024,1024]{1,0:T(8,128)(2,1)S(1)} %copy-done, f32[1568,1024]{1,0:T(8,128)S(1)} %get-tuple-element.97, f32[1024]{0:T(1024)S(1)} %copy-done.37, f32[1568]{0:T(1024)S(1)} %add_rsqrt_fusion.1, ...), kind=kOutput, calls=%fused_computation.50 | convolution fusion | flops 3399122944 | bytes 24592640 | tf_op jit(solution)/shard_map/dot_general | solution.py:13
  168.0 4.8 convolution_convert_fusion.1
  183.6 26.2 %all_gather.3 = bf16[1024,64]{0,1:T(8,128)(2,1)S(1)} all-gather(bf16[128,64]{0,1:T(8,128)(2,1)S(1)} %copy-done.38), channel_id=1, replica_groups=mesh['dp'=8,'mp'=4] {'dp'}, dimensions={0}, use_global_device_ids=true | all-gather | bytes 147456 | tf_op jit(solution)/shard_map/all_gather | solution.py:116
  209.8 32.8 %all-reduce.10.cloned.1.call-done = bf16[1568,1024]{1,0:T(8,128)(2,1)} async-done(((bf16[1568,1024]{1,0:T(8,128)(2,1)}), bf16[1568,1024]{1,0:T(8,128)(2,1)}) %all-reduce.10.cloned.1.call-update) | async-done | bytes 3211280 | tf_op jit(solution)/shard_map/psum | solution.py:112
  242.6 6.2 convert_reduce_fusion
  248.9 4.8 reshape.218
  267.4 6.1 reshape.219
  273.5 4.7 fusion.69
  279.9 4.6 fusion.19
  287.1 11.3 %add_convert_fusion.1 = bf16[1568,1024]{1,0:T(8,128)(2,1)S(1)} fusion(f32[1568,1024]{1,0:T(8,128)} %get-tuple-element.95, f32[1568,1024]{1,0:T(8,128)} %get-tuple-element.100, bf16[1024,1024]{1,0:T(8,128)(2,1)} %param.21, f32[1568,1024]{1,0:T(8,128)S(1)} %fusion.18), kind=kOutput, calls=%fused_computation.48 | convolution fusion | flops 3312418816 | bytes 24576000 | tf_op jit(solution)/shard_map/dot_general | solution.py:23
  300.1 5.2 convolution_convert_fusion
  305.4 9.3 %convolution_convert_fusion.7 = bf16[1024,1024]{1,0:T(8,128)(2,1)} fusion(bf16[1568,1024]{1,0:T(8,128)(2,1)} %copy-done.45, f32[1568,1024]{1,0:T(8,128)} %copy-done.7), kind=kOutput, calls=%fused_computation.87 | convolution fusion | flops 3290988544 | bytes 11730944 | tf_op jit(solution)/shard_map/dot_general | solution.py:17
  314.7 9.0 %convolution_convert_fusion.8 = bf16[1024,1024]{1,0:T(8,128)(2,1)} fusion(bf16[1568,1024]{1,0:T(8,128)(2,1)S(1)} %copy-done.44, f32[1568,1024]{1,0:T(8,128)} %copy-done.2, f32[1024]{0:T(1024)S(1)} %copy-done.37, f32[1568]{0:T(1024)S(1)} %add_rsqrt_fusion.1, f32[1568]{0:T(1024)S(1)} %broadcast_multiply_fusion.7), kind=kOutput, calls=%fused_computation.88 | convolution fusion | flops 3295805440 | bytes 11747584 | tf_op jit(solution)/shard_map/dot_general | solution.py:17
  323.7 51.4 %all-reduce.12.cloned.1.call-done = bf16[1568,1024]{1,0:T(8,128)(2,1)} async-done(((bf16[1568,1024]{1,0:T(8,128)(2,1)}), bf16[1568,1024]{1,0:T(8,128)(2,1)}) %all-reduce.12.cloned.1.call-update) | async-done | bytes 3211280 | tf_op jit(solution)/shard_map/psum | solution.py:152
  375.1 6.2 fusion.25
  381.3 5.9 fusion.23
  395.4 7.5 multiply_reduce_fusion
  402.9 6.4 multiply_convert_fusion
  418.4 4.9 fusion.93
  427.8 5.1 fusion.94
  437.4 7.9 %add_convert_fusion = bf16[1568,1024]{1,0:T(8,128)(2,1)} fusion(f32[1568,1024]{1,0:T(8,128)} %fusion.93, f32[1568,1024]{1,0:T(8,128)} %fusion.94, bf16[1568,256]{0,1:T(8,128)(2,1)} %reshape.223, bf16[1024,256]{1,0:T(8,128)(2,1)} %param.18), kind=kOutput, calls=%fused_computation.47 | convolution fusion | flops 826900480 | bytes 17383424 | tf_op jit(solution)/shard_map/dot_general | solution.py:23
  449.4 4.5 convolution_convert_fusion.11
  459.9 5.6 copy.128
  467.1 48.0 %all-reduce.14.cloned.1.call-done = bf16[1568,1024]{1,0:T(8,128)(2,1)} async-done(((bf16[1568,1024]{1,0:T(8,128)(2,1)}), bf16[1568,1024]{1,0:T(8,128)(2,1)}) %all-reduce.14.cloned.1.call-update) | async-done | bytes 3211280 | tf_op jit(solution)/shard_map/psum | solution.py:189
  515.1 6.2 fusion.31
  521.3 7.0 fusion.29
  532.8 5.4 copy.129
  538.2 23.2 %all-reduce = (bf16[1024]{0:T(1024)(128)(2,1)S(1)}, bf16[1024]{0:T(1024)(128)(2,1)S(1)}, bf16[1024]{0:T(1024)(128)(2,1)S(1)}, bf16[64,8]{0,1:T(8,128)(2,1)S(1)}) all-reduce(bf16[1024]{0:T(1024)(128)(2,1)S(1)} %get-tuple-element.74, bf16[1024]{0:T(1024)(128)(2,1)S(1)} %get-tuple-element.72, ...), channel_id=1, replica_groups=mesh['dp'=8,'mp'=4] {'dp'}, use_global_device_ids=true, to_apply=%region_29.30 | all-reduce | flops 3584 | bytes 14336 | tf_op jit(solution)/shard_map/psum | solution.py:213
  563.7 179.4 %all-reduce.16.cloned.1.call-done = (bf16[1024,256]{1,0:T(8,128)(2,1)}, bf16[1024,256]{1,0:T(8,128)(2,1)}, bf16[1024,256]{1,0:T(8,128)(2,1)}, bf16[256,1024]{1,0...) async-done(((bf16[1024,256]{1,0:T(8,128)(2,1)}, bf16[1024,256]{1,0:T(8,128)(2,1)}, bf16[1024,256]{1,0:T(8,128)(2,1)}, ...) | async-done | bytes 6422544 | tf_op jit(solution)/shard_map/psum | solution.py:209
  (200 shorter events, 145.2 us)
Async XLA Ops:
  7.2 139.4 %copy-start = (bf16[1024,1024]{1,0:T(8,128)(2,1)S(1)}, bf16[1024,1024]{1,0:T(8,128)(2,1)}, u32[]{:S(2)}) copy-start(bf16[1024,1024]{1,0:T(8,128)(2,1)} %param.20) | copy-start | bytes 6291460
  7.2 134.0 %all-reduce.8.cloned.1.call-start = ((), (), s32[]{:S(2)}) async-start(), calls=%async_computation | async-start | bytes 6422528 | tf_op jit(solution)/shard_map/psum | solution.py:107
  7.2 6.7 copy-start.6
  14.7 9.4 %copy-start.32 = (f32[1568]{0:T(1024)}, f32[1568]{0:T(1024)S(1)}, u32[]{:S(2)}) copy-start(f32[1568]{0:T(1024)S(1)} %div.55) | copy-start | bytes 18820
  14.7 10.0 %copy-start.36 = (f32[1024]{0:T(1024)S(1)}, f32[1024]{0:T(1024)}, u32[]{:S(2)}) copy-start(f32[1024]{0:T(1024)} %param.22) | copy-start | bytes 12292
  29.8 7.6 copy-start.30
  44.7 14.7 %copy-start.13 = (bf16[8,196,4,64]{1,3,2,0:T(8,128)(2,1)}, bf16[8,196,4,64]{1,3,2,0:T(8,128)(2,1)S(1)}, u32[]{:S(2)}) copy-start(bf16[8,196,4,64]{1,3,2,0:T(8,128)(2,1)S(1)} %copy.107) | copy-start | bytes 2408452
  44.7 11.8 %copy-start.40 = (s32[8,196]{1,0:T(8,128)S(1)}, s32[8,196]{1,0:T(8,128)}, u32[]{:S(2)}) copy-start(s32[8,196]{1,0:T(8,128)} %param.15) | copy-start | bytes 18820
  66.1 79.6 %copy-start.11 = (bf16[1568,256]{0,1:T(8,128)(2,1)}, bf16[1568,256]{0,1:T(8,128)(2,1)S(1)}, u32[]{:S(2)}) copy-start(bf16[1568,256]{0,1:T(8,128)(2,1)S(1)} %reshape.216) | copy-start | bytes 2408452
  68.9 173.8 %all-reduce.10.cloned.1.call-start = ((), (), s32[]{:S(2)}) async-start(), calls=%async_computation.1 | async-start | bytes 6422528 | tf_op jit(solution)/shard_map/psum | solution.py:112
  145.7 20.6 %copy-start.2 = (f32[1568,1024]{1,0:T(8,128)}, f32[1568,1024]{1,0:T(8,128)S(1)}, u32[]{:S(2)}) copy-start(f32[1568,1024]{1,0:T(8,128)S(1)} %get-tuple-element.97) | copy-start | bytes 19267588
  146.6 21.4 %copy-start.42 = (bf16[1024,1024]{1,0:T(8,128)(2,1)S(1)}, bf16[1024,1024]{1,0:T(8,128)(2,1)}, u32[]{:S(2)}) copy-start(bf16[1024,1024]{1,0:T(8,128)(2,1)} %param.21) | copy-start | bytes 6291460
  172.9 202.2 %all-reduce.12.cloned.1.call-start = ((), (), s32[]{:S(2)}) async-start(), calls=%async_computation.2 | async-start | bytes 6422528 | tf_op jit(solution)/shard_map/psum | solution.py:152
  175.6 7.9 %copy-start.38 = (bf16[128,64]{0,1:T(8,128)(2,1)S(1)}, bf16[128,64]{0,1:T(8,128)(2,1)}, u32[]{:S(2)}) copy-start(bf16[128,64]{0,1:T(8,128)(2,1)} %param.25) | copy-start | bytes 49156
  248.9 7.8 %copy-start.39 = (f32[1024]{0:T(1024)S(1)}, f32[1024]{0:T(1024)}, u32[]{:S(2)}) copy-start(f32[1024]{0:T(1024)} %param.24) | copy-start | bytes 12292
  287.1 11.3 %copy-start.7 = (f32[1568,1024]{1,0:T(8,128)}, f32[1568,1024]{1,0:T(8,128)S(1)}, u32[]{:S(2)}) copy-start(f32[1568,1024]{1,0:T(8,128)S(1)} %fusion.18) | copy-start | bytes 19267588
  305.3 209.8 %all-reduce.14.cloned.1.call-start = ((), (), s32[]{:S(2)}) async-start(), calls=%async_computation.3 | async-start | bytes 6422528 | tf_op jit(solution)/shard_map/psum | solution.py:189
  305.4 9.4 %copy-start.44 = (bf16[1568,1024]{1,0:T(8,128)(2,1)S(1)}, bf16[1568,1024]{1,0:T(8,128)(2,1)}, u32[]{:S(2)}) copy-start(bf16[1568,1024]{1,0:T(8,128)(2,1)} %copy-done.43) | copy-start | bytes 9633796
  381.3 8.7 %copy-start.26 = (bf16[256,1024]{1,0:T(8,128)(2,1)S(1)}, bf16[256,1024]{1,0:T(8,128)(2,1)}, u32[]{:S(2)}) copy-start(bf16[256,1024]{1,0:T(8,128)(2,1)} %param.19) | copy-start | bytes 1572868
  395.4 16.9 %slice-start = ((s8[6553600]{0:T(1024)(128)(4,1)}), s8[4194304]{0:T(1024)(128)(4,1)S(1)}, s32[]{:S(2)}) async-start(s8[6553600]{0:T(1024)(128)(4,1)} %bitcast.89), calls=%async_computation.5 | async-start | bytes 8388608
  402.9 6.5 copy-start.15
  402.9 7.2 copy-start.14
  402.9 9.4 %slice-start.1 = ((s8[6553600]{0:T(1024)(128)(4,1)}), s8[2359296]{0:T(1024)(128)(4,1)S(1)}, s32[]{:S(2)}) async-start(s8[6553600]{0:T(1024)(128)(4,1)} %bitcast.89), calls=%async_computation.6 | async-start | bytes 4718592
  445.3 297.7 %all-reduce.16.cloned.1.call-start = ((), (), s32[]{:S(2)}) async-start(), calls=%async_computation.4 | async-start | bytes 12845056 | tf_op jit(solution)/shard_map/psum | solution.py:209
  445.8 8.1 %copy-start.16 = (bf16[1568,256]{0,1:T(8,128)(2,1)S(1)}, bf16[1568,256]{0,1:T(8,128)(2,1)}, u32[]{:S(2)}) copy-start(bf16[1568,256]{0,1:T(8,128)(2,1)} %reshape.222) | copy-start | bytes 2408452
  445.9 8.1 %copy-start.21 = (bf16[1568,1024]{1,0:T(8,128)(2,1)S(1)}, bf16[1568,1024]{1,0:T(8,128)(2,1)}, u32[]{:S(2)}) copy-start(bf16[1568,1024]{1,0:T(8,128)(2,1)} %convert_element_type.246) | copy-start | bytes 9633796
  449.4 6.5 copy-start.20
  449.4 8.5 %slice-start.2 = ((s8[6422528]{0:T(1024)(128)(4,1)}), s8[4194304]{0:T(1024)(128)(4,1)S(1)}, s32[]{:S(2)}) async-start(s8[6422528]{0:T(1024)(128)(4,1)} %bitcast.91), calls=%async_computation.7 | async-start | bytes 8388608
  459.9 55.2 %copy-start.33 = (f32[1568]{0:T(1024)S(1)}, f32[1568]{0:T(1024)}, u32[]{:S(2)}) copy-start(f32[1568]{0:T(1024)} %copy-done.32) | copy-start | bytes 18820
  459.9 55.2 %copy-start.35 = (f32[1568]{0:T(1024)S(1)}, f32[1568]{0:T(1024)}, u32[]{:S(2)}) copy-start(f32[1568]{0:T(1024)} %copy-done.34) | copy-start | bytes 18820
  743.1 8.5 %copy-start.24 = (bf16[1024,1024]{1,0:T(8,128)(2,1)S(1)}, bf16[1024,1024]{1,0:T(8,128)(2,1)}, u32[]{:S(2)}) copy-start(bf16[1024,1024]{1,0:T(8,128)(2,1)} %get-tuple-element.87) | copy-start | bytes 6291460
  743.1 11.0 %copy-start.23 = (bf16[1024,1024]{1,0:T(8,128)(2,1)S(1)}, bf16[1024,1024]{1,0:T(8,128)(2,1)}, u32[]{:S(2)}) copy-start(bf16[1024,1024]{1,0:T(8,128)(2,1)} %get-tuple-element.88) | copy-start | bytes 6291460
  (25 other events, 99.0 us)
Sparse Core Ops, SparseCore 0:
  69.0 72.1 all-reduce.7
  173.0 69.5 all-reduce.9
  305.4 69.5 all-reduce.11
  445.5 69.5 all-reduce.13
  521.1 221.9 all-reduce.15
where the time goes:
time: 769 us; the launch traced here: 765 us
  waiting for transfers between devices  384 us (50%)
  matrix products  140 us (18%)
  local copies, waits for them, and re-layouts  95.1 us (12%)
  other arithmetic  80.6 us (10%)
  blocking collectives  49.4 us (6%)
  between operations  14.7 us (2%)
    psum x1, waiting for transfers between devices, local(): lax.psum(grad_query.astype(jnp.bfloat16), 'dp').astype(jnp.float32)  179 us
    psum x1, waiting for transfers between devices, local(): lax.psum(attn_term.astype(jnp.bfloat16), 'mp').astype(jnp.float32)  72.3 us
    psum x1, waiting for transfers between devices, local(): lax.psum(mlp_back_term.astype(jnp.bfloat16), 'mp').astype(jnp.float32)  51.4 us
    psum x1, waiting for transfers between devices, local(): lax.psum(attn_terms.astype(jnp.bfloat16), 'mp').astype(jnp.float32)  48 us
    dot_general x8, matrix products, contract_cols(): lax.dot_general(left, right, (((1,), (1,)), ((), ())), preferred_element_...  41.6 us
    dot_general x8, matrix products, product(): return jnp.dot(left, right, preferred_element_type=jnp.float32)  39.4 us
    psum x1, waiting for transfers between devices, local(): lax.psum(product(activated, w_down).astype(jnp.bfloat16), 'mp')  32.8 us
    dot_general x8, matrix products, contract_rows(): lax.dot_general(left, right, (((0,), (0,)), ((), ())), preferred_element_...  32.4 us
  transfers between devices with their start and end apart: 5, of which 5 were waited for; matrix products, arithmetic and copies ran while one was open for 10% of the time, Pallas kernels for 0%

commit v1 on v0

--- a/solution.py
+++ b/solution.py
@@ -3,6 +3,8 @@
 import jax
 import jax.numpy as jnp
 from jax import lax
+from jax.experimental import pallas as pl
+from jax.experimental.pallas import tpu as pltpu
 from jax.sharding import PartitionSpec as P
 
 D = 1024
@@ -240,9 +242,496 @@
     )
 
 
+MESH = pl.DeviceIdType.MESH
+PAD = 208
+CH = 16
+TILE = 256
+f32 = jnp.float32
+bf16 = jnp.bfloat16
+
+
+def nn(a, b):
+    return jnp.dot(a, b, preferred_element_type=f32)
+
+
+def nt(a, b):
+    return lax.dot_general(a, b, (((1,), (1,)), ((), ())), preferred_element_type=f32)
+
+
+def tn(a, b):
+    return lax.dot_general(a, b, (((0,), (0,)), ((), ())), preferred_element_type=f32)
+
+
+def gauss(z):
+    bell = jnp.exp(-0.5 * (z * z))
+    t = 1.0 / (1.0 + 0.23164189 * jnp.abs(z))
+    poly = t * (
+        0.127414796 + t * (-0.142248368 + t * (0.7107068705 + t * (-0.7265760135 + t * 0.5307027145)))
+    )
+    tail = poly * bell
+    return jnp.where(z >= 0, 1.0 - tail, tail), 0.3989422804014327 * bell
+
+
+def stats(v):
+    mean = jnp.sum(v, axis=-1, keepdims=True) * (1.0 / v.shape[-1])
+    c = v - mean
+    s = lax.rsqrt(jnp.sum(c * c, axis=-1, keepdims=True) * (1.0 / v.shape[-1]) + 1e-06)
+    return c * s, s
+
+
+def back(e, u, s):
+    width = 1.0 / e.shape[-1]
+    return s * (
+        e
+        - jnp.sum(e, axis=-1, keepdims=True) * width
+        - u * (jnp.sum(e * u, axis=-1, keepdims=True) * width)
+    )
+
+
+def fold(v):
+    total = v[0:8]
+    for r in range(8, v.shape[0], 8):
+        total = total + v[r : r + 8]
+    return total
+
+
+def chunks():
+    return range(0, PAD, CH)
+
+
+def fused(
+    patches, bias_hbm, wq_hbm, wk_hbm, wv_hbm, wo_hbm, wup_hbm, wdn_hbm, g1_ref, g2_ref, g3_ref,
+    wl_hbm, wsel_ref, ct_ref,
+    learned_ref, y_hbm, gp_hbm, gup_hbm, gdn_hbm, gout_hbm, gqkv_hbm, dg_ref, gl_ref, gsel_ref,
+    xraw, bias, wqkv, wo, wup, wdn, wl,
+    xs, qkv, os, h1s, a2s, rs, gs, dhs, d1s,
+    pbuf, rcore, tbuf, rx, sumb, gst,
+    sx, sw, sy, sg, slearn_s, slearn_r, s_core, r_core, s_x, r_x, s_ag, r_ag,
+):
+    images = patches.shape[0]
+    count = patches.shape[1]
+    width = patches.shape[2]
+    half = width // 2
+    dp = lax.axis_index("dp")
+    mp = lax.axis_index("mp")
+    core = lax.rem(mp, 2)
+    mate = (dp, mp + 1 - 2 * core)
+    across = (dp, lax.rem(mp + 2, 4))
+    dps = lax.axis_size("dp")
+    lrows = wl_hbm.shape[0]
+
+    barrier = pltpu.get_barrier_semaphore()
+    for device in (mate, across):
+        pl.semaphore_signal(barrier, inc=1, device_id=device, device_id_type=MESH)
+    for k in range(1, dps):
+        pl.semaphore_signal(barrier, inc=1, device_id=(lax.rem(dp + k, dps), mp), device_id_type=MESH)
+
+    loads = [
+        pltpu.make_async_copy(wq_hbm, wqkv.at[:, pl.ds(0, 256)], sw.at[0]),
+        pltpu.make_async_copy(wk_hbm, wqkv.at[:, pl.ds(256, 256)], sw.at[1]),
+        pltpu.make_async_copy(wv_hbm, wqkv.at[:, pl.ds(512, 256)], sw.at[2]),
+        pltpu.make_async_copy(wo_hbm, wo, sw.at[3]),
+        pltpu.make_async_copy(wup_hbm, wup, sw.at[4]),
+        pltpu.make_async_copy(wdn_hbm, wdn, sw.at[5]),
+        pltpu.make_async_copy(wl_hbm, wl.at[dp], sw.at[6]),
+        pltpu.make_async_copy(bias_hbm, bias, sw.at[7]),
+    ]
+
+    def load_x(i, slot):
+        return pltpu.make_async_copy(patches.at[i], xraw.at[slot], sx.at[slot])
+
+    load_x(0, 0).start()
+    for k in (0, 1, 2, 7, 3):
+        loads[k].start()
+    load_x(1, 1).start()
+    for k in (6, 4, 5):
+        loads[k].start()
+
+    xs[...] = jnp.zeros_like(xs)
+
+    pl.semaphore_wait(barrier, dps + 1)
+
+    def learn_copy(k):
+        return pltpu.make_async_remote_copy(
+            src_ref=wl.at[dp], dst_ref=wl.at[dp],
+            send_sem=slearn_s.at[k - 1], recv_sem=slearn_r.at[k - 1],
+            device_id=(lax.rem(dp + k, dps), mp), device_id_type=MESH,
+        )
+
+    loads[6].wait()
+    for k in range(1, dps):
+        learn_copy(k).start()
+
+    g1 = g1_ref[...]
+    g2 = g2_ref[...]
+    g3 = g3_ref[...]
+    lane_head = lax.broadcasted_iota(jnp.int32, (1, 256), 1) // 64
+
+    def only(v, h):
+        return jnp.where(lane_head == h, v, jnp.zeros_like(v))
+
+    def rows_of(i):
+        return pl.ds(pl.multiple_of(i * PAD, 16), PAD)
+
+    def chunk_of(i, r):
+        return pl.ds(pl.multiple_of(i * PAD + r, 16), CH)
+
+    def copy_core(i):
+        return pltpu.make_async_remote_copy(
+            src_ref=pbuf.at[1 - core, rows_of(i)], dst_ref=rcore.at[rows_of(i)],
+            send_sem=s_core.at[i], recv_sem=r_core.at[i], device_id=mate, device_id_type=MESH,
+        )
+
+    def copy_x(i, par):
+        return pltpu.make_async_remote_copy(
+            src_ref=tbuf.at[rows_of(i)], dst_ref=rx.at[par, rows_of(i)],
+            send_sem=s_x.at[i], recv_sem=r_x.at[par, i], device_id=across, device_id_type=MESH,
+        )
+
+    def copy_ag(i):
+        return pltpu.make_async_remote_copy(
+            src_ref=sumb.at[core, rows_of(i)], dst_ref=sumb.at[core, rows_of(i)],
+            send_sem=s_ag.at[i], recv_sem=r_ag.at[i], device_id=mate, device_id_type=MESH,
+        )
+
+    def hop_two(i, par):
+        copy_core(i).wait()
+        rows = rows_of(i)
+        tbuf[rows] = (pbuf[core, rows].astype(f32) + rcore[rows].astype(f32)).astype(bf16)
+        copy_x(i, par).start()
+
+    def hop_three(i, par):
+        copy_x(i, par).wait()
+        rows = rows_of(i)
+        sumb[core, rows] = (tbuf[rows].astype(f32) + rx[par, rows].astype(f32)).astype(bf16)
+        copy_ag(i).start()
+
+    def arrived(i):
+        copy_ag(i).wait()
+
+    def summed(i, r):
+        where = chunk_of(i, r)
+        return jnp.concatenate([sumb[0, where].astype(f32), sumb[1, where].astype(f32)], axis=1)
+
+    def store_p(i, t, value):
+        pbuf[t // 2, rows_of(i), (t % 2) * TILE : (t % 2 + 1) * TILE] = value.astype(bf16)
+
+    def stage(body, par, first=False):
+        def step(i, carry):
+            if not first:
+                @pl.when(i + 1 < images)
+                def _():
+                    hop_three(i + 1, 1 - par)
+                arrived(i)
+            body(i)
+            copy_core(i).start()
+
+            @pl.when(i > 0)
+            def _():
+                hop_two(i - 1, par)
+            return carry
+
+        if not first:
+            hop_three(0, 1 - par)
+        lax.fori_loop(0, images, step, 0)
+        hop_two(images - 1, par)
+
+    for k in (0, 1, 2, 3, 7):
+        loads[k].wait()
+
+    def attention(i):
+        slot = lax.rem(i, 2)
+        load_x(i, slot).wait()
+        start = pl.multiple_of(i * PAD, 16)
+        xs[pl.ds(start, count), :] = xraw[slot]
+
+        @pl.when(i + 2 < images)
+        def _():
+            load_x(i + 2, slot).start()
+
+        for r in chunks():
+            u, _ = stats(xs[chunk_of(i, r), :].astype(f32))
+            a2s[chunk_of(i, r), :] = (u * g1).astype(bf16)
+        rows = rows_of(i)
+        a1 = a2s[rows, :]
+        qkv[rows, 0:256] = (nn(a1, wqkv[:, 0:256]) * 0.125).astype(bf16)
+        qkv[rows, 256:512] = nn(a1, wqkv[:, 256:512]).astype(bf16)
+        qkv[rows, 512:768] = nn(a1, wqkv[:, 512:768]).astype(bf16)
+        q = qkv[rows, 0:256]
+        k = qkv[rows, 256:512]
+        v = qkv[rows, 512:768]
+        row_bias = bias[i]
+        o = jnp.zeros((PAD, 256), f32)
+        for h in range(4):
+            scores = nt(only(q, h), k) + row_bias
+            e = jnp.exp(scores - jnp.max(scores, axis=1, keepdims=True))
+            p = (e * (1.0 / jnp.sum(e, axis=1, keepdims=True))).astype(bf16)
+            o = o + nn(p, only(v, h))
+        ob = o.astype(bf16)
+        os[rows, :] = ob
+        for t in range(4):
+            store_p(i, t, nn(ob, wo[:, t * TILE : (t + 1) * TILE]))
+
+    stage(attention, 0, first=True)
+
+    loads[4].wait()
+    loads[5].wait()
+
+    def mlp(i):
+        for r in chunks():
+            h1 = xs[chunk_of(i, r), :].astype(f32) + summed(i, r)
+            h1s[chunk_of(i, r), :] = h1
+            u, _ = stats(h1)
+            a2s[chunk_of(i, r), :] = (u * g2).astype(bf16)
+        rows = rows_of(i)
+        a2 = a2s[rows, :]
+        for t in range(4):
+            cols = slice(t * TILE, (t + 1) * TILE)
+            z = nn(a2, wup[:, cols])
+            cdf, pdf = gauss(z)
+            rs[rows, cols] = (z * cdf).astype(bf16)
+            gs[rows, cols] = (cdf + z * pdf).astype(bf16)
+        act = rs[rows, :]
+        for t in range(4):
+            store_p(i, t, nn(act, wdn[:, t * TILE : (t + 1) * TILE]))
+
+    stage(mlp, 1)
+
+    for k in range(1, dps):
+        learn_copy(k).wait()
+    dg_ref[...] = jnp.zeros_like(dg_ref)
+    gl_ref[...] = jnp.zeros_like(gl_ref)
+    gsel_ref[...] = jnp.zeros_like(gsel_ref)
+
+    def y_out(i):
+        return pltpu.make_async_copy(d1s.at[rows_of(i)], y_hbm.at[rows_of(i)], sy.at[i])
+
+    def learner(i):
+        rows = rows_of(i)
+        for r in chunks():
+            yb = (h1s[chunk_of(i, r), :] + summed(i, r)).astype(bf16)
+            d1s[chunk_of(i, r), :] = yb
+            u, _ = stats(yb.astype(f32))
+            dhs[chunk_of(i, r), :] = (u * g3).astype(bf16)
+        y_out(i).start()
+        y = d1s[rows, :]
+        a3 = dhs[rows, :]
+        wlf = wl[...].reshape(width, wl.shape[2])
+        wsel = wsel_ref[...]
+        ct = ct_ref[i]
+        zl = nn(a3, wlf)
+        cdf, pdf = gauss(zl)
+        t = (zl * cdf).astype(bf16)
+        slope = cdf + zl * pdf
+        eye = lax.broadcasted_iota(jnp.int32, (PAD, PAD), 0) == lax.broadcasted_iota(jnp.int32, (PAD, PAD), 1)
+        col_bias = jnp.sum(jnp.where(eye, bias[i], 0.0), axis=1, keepdims=True)
+        logits = nn(t, wsel) + col_bias
+        e = jnp.exp(logits - jnp.max(logits, axis=0, keepdims=True))
+        maps = e * (1.0 / jnp.sum(e, axis=0, keepdims=True))
+        mb = maps.astype(bf16)
+        learned_ref[i] = tn(mb, y).astype(bf16)
+        dmaps = nt(y, ct)
+        dlog = (maps * (dmaps - jnp.sum(maps * dmaps, axis=0, keepdims=True))).astype(bf16)
+        gsel_ref[...] += tn(t, dlog)
+        dzl = (nt(dlog, wsel) * slope).astype(bf16)
+        gl_ref[...] += tn(a3, dzl)
+        for r in chunks():
+            da3 = nt(dzl[r : r + CH], wlf)
+            dy = nn(mb[r : r + CH], ct)
+            u, s = stats(d1s[chunk_of(i, r), :].astype(f32))
+            dg_ref[2] += fold(da3 * u)
+            dhs[chunk_of(i, r), :] = (dy + back(da3 * g3, u, s)).astype(bf16)
+        dhb = dhs[rows, :]
+        for c in range(4):
+            cols = slice(c * TILE, (c + 1) * TILE)
+            dr = nt(dhb, wdn[cols, :])
+            gs[rows, cols] = (dr * gs[rows, cols].astype(f32)).astype(bf16)
+        dz = gs[rows, :]
+        for c in range(4):
+            store_p(i, c, nt(dz, wup[c * TILE : (c + 1) * TILE, :]))
+
+    stage(learner, 0)
+
+    def grad(left, right, ntile, out, col0, slot0):
+        wide = right.shape[1]
+
+        def g_out(j, slot):
+            return pltpu.make_async_copy(
+                gst.at[slot, :, pl.ds(0, wide)], out.at[pl.ds(pl.multiple_of(j * TILE, 16), TILE)], sg.at[slot]
+            )
+
+        def step(j, carry):
+            slot = lax.rem(j, 2)
+
+            @pl.when(j >= 2)
+            def _():
+                g_out(j - 2, slot).wait()
+
+            lhs = left[:, pl.ds(pl.multiple_of(j * TILE, TILE), TILE)]
+            for c in range(0, wide, TILE):
+                gst[slot, :, c : c + TILE] = tn(lhs, right[:, c : c + TILE]).astype(bf16)
+            g_out(j, slot).start()
+            return carry
+
+        lax.fori_loop(0, ntile, step, 0)
+        for j in range(max(ntile - 2, 0), ntile):
+            g_out(j, j % 2).wait()
+
+    grad(rs, dhs, 4, gdn_hbm, 0, 0)
+    grad(a2s, gs, 4, gup_hbm, 0, 0)
+
+    for i in range(images):
+        y_out(i).wait()
+
+    def attention_back(i):
+        rows = rows_of(i)
+        for r in chunks():
+            where = chunk_of(i, r)
+            da2 = summed(i, r)
+            u, s = stats(h1s[where, :])
+            dg_ref[1] += fold(da2 * u)
+            d1s[where, :] = (dhs[where, :].astype(f32) + back(da2 * g2, u, s)).astype(bf16)
+            ux, _ = stats(xs[where, :].astype(f32))
+            a2s[where, :] = (ux * g1).astype(bf16)
+        d1 = d1s[rows, :]
+        do = nt(d1, wo[...]).astype(bf16)
+        q = qkv[rows, 0:256]
+        k = qkv[rows, 256:512]
+        v = qkv[rows, 512:768]
+        eye = lax.broadcasted_iota(jnp.int32, (PAD, PAD), 0) == lax.broadcasted_iota(jnp.int32, (PAD, PAD), 1)
+        col_bias = jnp.sum(jnp.where(eye, bias[i], 0.0), axis=1, keepdims=True)
+        dq = jnp.zeros((PAD, 256), f32)
+        dk = jnp.zeros((PAD, 256), f32)
+        dv = jnp.zeros((PAD, 256), f32)
+        for h in range(4):
+            kh = only(k, h)
+            scores = nt(kh, q) + col_bias
+            e = jnp.exp(scores - jnp.max(scores, axis=0, keepdims=True))
+            p = e * (1.0 / jnp.sum(e, axis=0, keepdims=True))
+            dv = dv + nn(p.astype(bf16), only(do, h))
+            dpr = nt(only(v, h), do)
+            ds = (p * (dpr - jnp.sum(p * dpr, axis=0, keepdims=True))).astype(bf16)
+            dk = dk + nn(ds, only(q, h))
+            dq = dq + tn(ds, kh)
+        qkv[rows, 0:256] = (dq * 0.125).astype(bf16)
+        qkv[rows, 256:512] = dk.astype(bf16)
+        qkv[rows, 512:768] = dv.astype(bf16)
+        dall = qkv[rows, :]
+        for c in range(4):
+            store_p(i, c, nt(dall, wqkv[c * TILE : (c + 1) * TILE, :]))
+
+    stage(attention_back, 1)
+    grad(os, d1s, 1, gout_hbm, 0, 0)
+    grad(a2s, qkv, 4, gqkv_hbm, 0, 0)
+
+    def gp_out(i):
+        return pltpu.make_async_copy(rs.at[rows_of(i)], gp_hbm.at[rows_of(i)], sy.at[i])
+
+    def finish(i, carry):
+        @pl.when(i + 1 < images)
+        def _():
+            hop_three(i + 1, 1)
+        arrived(i)
+        for r in chunks():
+            where = chunk_of(i, r)
+            da1 = summed(i, r)
+            u, s = stats(xs[where, :].astype(f32))
+            dg_ref[0] += fold(da1 * u)
+            rs[where, :] = (d1s[where, :].astype(f32) + back(da1 * g1, u, s)).astype(bf16)
+        gp_out(i).start()
+        return carry
+
+    hop_three(0, 1)
+    lax.fori_loop(0, images, finish, 0)
+    for i in range(images):
+        gp_out(i).wait()
+
+
+def local_fused(
+    patches, keep_mask, w_query, w_key, w_value, w_out, w_up, w_down,
+    gain_attn, gain_mlp, gain_learn, w_learn, w_select, cotangent,
+):
+    images, count, width = patches.shape
+    total = images * PAD
+    hidden = w_up.shape[1]
+    bias = jnp.where(jnp.pad(keep_mask, ((0, 0), (0, PAD - count))) > 0, 0.0, -1e30).astype(f32)[:, None, :]
+    learn_rows, learn_cols = w_learn.shape
+    dps = lax.axis_size("dp")
+    anywhere = pl.BlockSpec(memory_space=pl.ANY)
+    vmem = pl.BlockSpec(memory_space=pltpu.VMEM)
+    sds = jax.ShapeDtypeStruct
+    dma = pltpu.SemaphoreType.DMA
+    outs = pl.pallas_call(
+        fused,
+        name="block",
+        out_shape=(
+            sds((images, 8, width), bf16),
+            sds((total, width), bf16),
+            sds((total, width), bf16),
+            sds((width, hidden), bf16),
+            sds((hidden, width), bf16),
+            sds((256, width), bf16),
+            sds((width, 768), bf16),
+            sds((3, 8, width), f32),
+            sds((width, learn_cols), f32),
+            sds((learn_cols, 8), f32),
+        ),
+        in_specs=[anywhere] * 8 + [vmem] * 3 + [anywhere] + [vmem] * 2,
+        out_specs=(vmem,) + (anywhere,) * 6 + (vmem,) * 3,
+        scratch_shapes=[
+            pltpu.VMEM((2, count, width), bf16),
+            pltpu.VMEM((images, 1, PAD), f32),
+            pltpu.VMEM((width, 768), bf16),
+            pltpu.VMEM((256, width), bf16),
+            pltpu.VMEM((width, hidden), bf16),
+            pltpu.VMEM((hidden, width), bf16),
+            pltpu.VMEM((dps, learn_rows, learn_cols), bf16),
+            pltpu.VMEM((total, width), bf16),
+            pltpu.VMEM((total, 768), bf16),
+            pltpu.VMEM((total, 256), bf16),
+            pltpu.VMEM((total, width), f32),
+            pltpu.VMEM((total, width), bf16),
+            pltpu.VMEM((total, hidden), bf16),
+            pltpu.VMEM((total, hidden), bf16),
+            pltpu.VMEM((total, width), bf16),
+            pltpu.VMEM((total, width), bf16),
+            pltpu.VMEM((2, total, width // 2), bf16),
+            pltpu.VMEM((total, width // 2), bf16),
+            pltpu.VMEM((total, width // 2), bf16),
+            pltpu.VMEM((2, total, width // 2), bf16),
+            pltpu.VMEM((2, total, width // 2), bf16),
+            pltpu.VMEM((2, TILE, width), bf16),
+            dma((2,)), dma((8,)), dma((images,)), dma((2,)), dma((dps - 1,)), dma((dps - 1,)),
+            dma((images,)), dma((images,)), dma((images,)), dma((2, images)), dma((images,)), dma((images,)),
+        ],
+        compiler_params=pltpu.CompilerParams(
+            collective_id=0, has_side_effects=True, vmem_limit_bytes=60 * 2**20
+        ),
+    )(
+        patches, bias, w_query, w_key, w_value, w_out, w_up, w_down,
+        gain_attn[None], gain_mlp[None], gain_learn[None], w_learn, w_select, cotangent,
+    )
+    learned, y, gpat, gup, gdn, gout, gqkv, dg, gl, gsel = outs
+    y = y.reshape(images, PAD, width)[:, :count]
+    gpat = gpat.reshape(images, PAD, width)[:, :count]
+
+    def over_dp(v):
+        return lax.psum(v.astype(bf16), "dp").astype(f32)
+
+    gup, gdn, gout, gqkv = over_dp(gup), over_dp(gdn), over_dp(gout), over_dp(gqkv)
+    dg = over_dp(jnp.sum(dg, axis=1))
+    gl, gsel = over_dp(gl), over_dp(gsel)
+    gl = lax.dynamic_slice_in_dim(gl, lax.axis_index("dp") * learn_rows, learn_rows, 0)
+    return (
+        learned, y, gpat, gqkv[:, :256], gqkv[:, 256:512], gqkv[:, 512:], gout, gup, gdn,
+        dg[0], dg[1], dg[2], gl, gsel,
+    )
+
+
 def solution(mesh):
+    small = mesh.shape["dp"] == 8 and mesh.shape["mp"] == 4
     return jax.shard_map(
-        local,
+        local_fused if small else local,
         mesh=mesh,
         in_specs=(
             P("dp", None, None),

time: 769 us -> 422 us (0.55)
  waiting for transfers between devices: 384 us -> 173 us
  Pallas kernels: 0 us -> 163 us
  matrix products: 140 us -> 0 us
  local copies, waits for them, and re-layouts: 95.1 us -> 23.7 us
  other arithmetic: 80.6 us -> 10.5 us
  blocking collectives: 49.4 us -> 36.9 us
    psum x5 -> x1, waiting for transfers between devices: 384 us -> 173 us  [over_dp(): return lax.psum(v.astype(bf16), 'dp').astype(f32)]
    pallas_call x0 -> x1, Pallas kernels: none -> 163 us  [local_fused(): pl.pallas_call(fused, name='block', out_shape=(sds((images, 8, width), bf...]
    dot_general x32 -> x0, matrix products: 136 us -> none  [the longest x8 41.6 us: contract_cols(): lax.dot_general(left, right, (((1,), (1,)), ((), ())), preferred_element_...]
    reshape x16 -> x0, local copies, waits for them, and re-layouts: 47.7 us -> none  [the longest x2 7.46 us: local(): key_heads = key_flat.reshape(head_shape)]
    reduce_sum x9 -> x1, other arithmetic: 31.4 us -> 0.04 us  [local_fused(): dg = over_dp(jnp.sum(dg, axis=1))]
    convert_element_type x16 -> x6, other arithmetic: 39.4 us -> 9.74 us  [over_dp(): return lax.psum(v.astype(bf16), 'dp').astype(f32)]
    convert_element_type x10 -> x0, local copies, waits for them, and re-layouts: 27.2 us -> none  [the longest x2 12.9 us: local(): patches.reshape(row_count, feature_count).astype(jnp.float32)]
    all_gather x1 -> x0, blocking collectives: 26.2 us -> none  [local(): learn_full = lax.all_gather(w_learn, 'dp', axis=0, tiled=True)]
  transfers between devices with their start and end apart: 5 -> 1, of which waited for: 5 -> 1; matrix products, arithmetic and copies ran while one was open for 10% -> 2% of each run, Pallas kernels for 0% -> 0%
where the time goes in v1:
time: 422 us
  waiting for transfers between devices  173 us (41%)
  Pallas kernels  163 us (39%)
  blocking collectives  36.9 us (9%)
  local copies, waits for them, and re-layouts  23.7 us (6%)
  between operations  14.1 us (3%)
  other arithmetic  10.5 us (2%)
    psum x1, waiting for transfers between devices, over_dp(): return lax.psum(v.astype(bf16), 'dp').astype(f32)  173 us
    pallas_call x1, Pallas kernels, local_fused(): pl.pallas_call(fused, name='block', out_shape=(sds((images, 8, width), bf...  163 us
    psum x1, blocking collectives, over_dp(): return lax.psum(v.astype(bf16), 'dp').astype(f32)  36.9 us
    unnamed x24, local copies, waits for them, and re-layouts  20.1 us
    convert_element_type x6, other arithmetic, over_dp(): return lax.psum(v.astype(bf16), 'dp').astype(f32)  9.74 us
  transfers between devices with their start and end apart: 1, of which 1 were waited for; matrix products, arithmetic and copies ran while one was open for 2% of the time, Pallas kernels for 0%

profile of v1, /device:TPU:0, one launch (start us, length us, event | category | flops | bytes accessed | tf_op | source)
XLA Modules:
  0.0 421.7 jit_solution(8748783892890227319)
XLA Ops:
  7.2 0.0 all-reduce.5.cloned.1.call-start
  7.2 0.7 fusion
  7.9 0.6 broadcast_in_dim.22.bias_hbm
  8.5 1.4 copy.30.wsel_ref
  9.9 1.4 copy.29.wl_hbm
  11.3 5.4 %copy.28.patches = bf16[8,196,1024]{2,1,0:T(8,128)(2,1)} copy(bf16[8,196,1024]{2,0,1:T(8,128)(2,1)} %param.14) | data formatting | bytes 6422528 | tf_op args[0]
  16.7 163.1 %block.1 = (bf16[8,8,1024]{2,1,0:T(8,128)(2,1)}, bf16[1664,1024]{1,0:T(8,128)(2,1)}, bf16[1664,1024]{1,0:T(8,128)(2,1)}, bf16[1024,1024]{1,0:T(8,128)(2,1)}, bf1...) custom-call(bf16[8,196,1024]{2,1,0:T(8,128)(2,1)} %copy.28.patches, ...), custom_call_target="tpu_custom_call" | custom-call | tf_op jit(solution)/shard_map/block/pallas_call | solution.py:664
  179.8 1.8 convert_element_type.36
  181.6 0.0 all-reduce.5.cloned.1.call-update
  181.6 1.9 copy-done.2
  183.6 0.4 slice.32
  183.9 0.0 copy-start.7
  183.9 0.0 copy-start.6
  184.0 0.0 copy-start.1
  184.0 3.5 copy.35
  187.4 0.0 copy-done.7
  187.4 0.0 copy-done.6
  187.5 36.9 %all-reduce.1 = (bf16[3,1024]{1,0:T(4,128)(2,1)S(1)}, bf16[64,8]{1,0:T(8,128)(2,1)S(1)}) all-reduce(bf16[3,1024]{1,0:T(4,128)(2,1)S(1)} %reduce_sum.9, bf16[64,8]{1,0:T(8,128)(2,1)S(1)} %convert_element_type.38), channel_id=1, replica_groups=mesh['dp'=8,'mp'=4] {'dp'}, use_global_device_ids=true, to_apply=%region_5.6 | all-reduce | flops 3584 | bytes 14336 | tf_op jit(solution)/shard_map/psum | solution.py:719
  224.4 0.7 copy.34
  225.0 0.0 copy-done.1
  225.0 0.4 slice.33
  225.4 3.5 copy.36
  228.9 0.6 fusion.2
  229.5 173.4 %all-reduce.5.cloned.1.call-done = (bf16[1024,768]{1,0:T(8,128)(2,1)}, bf16[256,1024]{1,0:T(8,128)(2,1)}, bf16[1024,1024]{1,0:T(8,128)(2,1)}, bf16[1024,1024]{1,0:T(8,128)(2,1)}, bf16[1024,64]{1,0:T(8,128)(2,1)}) async-done(((bf16[1024,768]{1,0:T(8,128)(2,1)}, bf16[256,1024]{1,0:T(8,128)(2,1)}, bf16[1024,1024]{1,0:T(8,128)(2,1)}, bf16[1024,1024]{1,0:T(8,128)(2,1)}, bf16[1024,64]{1,0:T(8,128)(2,1)}), ...) | async-done | bytes 6422544 | tf_op jit(solution)/shard_map/psum | solution.py:719
  402.8 0.9 dynamic-slice_convert_fusion
  403.7 0.7 copy.33
  404.4 2.1 convert_element_type.31
  406.6 1.7 fusion.1
  408.3 1.0 copy-done.4
  409.3 2.5 convert_element_type.32
  411.8 2.5 convert_element_type.33
  414.2 0.7 copy.43
  (10 shorter events, 0.1 us)
Async XLA Ops:
  7.2 395.7 %all-reduce.5.cloned.1.call-start = ((), (), s32[]{:S(2)}) async-start(), calls=%async_computation | async-start | bytes 13107200 | tf_op jit(solution)/shard_map/psum | solution.py:719
  181.6 2.0 copy-start.2
  183.9 3.5 copy-start.7
  183.9 3.5 copy-start.6
  184.0 41.1 %copy-start.1 = (bf16[1664,1024]{1,0:T(8,128)(2,1)S(1)}, bf16[1664,1024]{1,0:T(8,128)(2,1)}, u32[]{:S(2)}) copy-start(bf16[1664,1024]{1,0:T(8,128)(2,1)} %get-tuple-element.26) | copy-start | bytes 10223620
  402.8 3.7 copy-start
  406.6 2.7 copy-start.4
  408.3 3.5 copy-start.3
  411.8 2.5 copy-start.5
Sparse Core Ops, SparseCore 0:
  181.7 221.0 all-reduce.4

commit v2 on v1

--- a/solution.py
+++ b/solution.py
@@ -246,6 +246,8 @@
 PAD = 208
 CH = 16
 TILE = 256
+PAIR_IN = 224
+LAG = 2
 f32 = jnp.float32
 bf16 = jnp.bfloat16
 
@@ -302,11 +304,12 @@
 def fused(
     patches, bias_hbm, wq_hbm, wk_hbm, wv_hbm, wo_hbm, wup_hbm, wdn_hbm, g1_ref, g2_ref, g3_ref,
     wl_hbm, wsel_ref, ct_ref,
-    learned_ref, y_hbm, gp_hbm, gup_hbm, gdn_hbm, gout_hbm, gqkv_hbm, dg_ref, gl_ref, gsel_ref,
-    xraw, bias, wqkv, wo, wup, wdn, wl,
-    xs, qkv, os, h1s, a2s, rs, gs, dhs, d1s,
-    pbuf, rcore, tbuf, rx, sumb, gst,
-    sx, sw, sy, sg, slearn_s, slearn_r, s_core, r_core, s_x, r_x, s_ag, r_ag,
+    learned_ref, y_hbm, gp_hbm, gall_hbm, small_ref, gl_ref,
+    xraw, bias, wqkv, wo, wl,
+    xs, qkv, os, h1s, a2s, dhs, d1s, big, recv,
+    pbuf, rcore, rx, sumb, dg, gl_sum, gsel_sum, gl_mine, gl_in, small_mine, small_in,
+    sx, sw, sy, slearn_s, slearn_r, s_core, r_core, s_x, r_x, s_ag, r_ag,
+    s_pair, r_pair, s_out, ready_y, ready_z, s_small, r_small,
 ):
     images = patches.shape[0]
     count = patches.shape[1]
@@ -318,7 +321,20 @@
     mate = (dp, mp + 1 - 2 * core)
     across = (dp, lax.rem(mp + 2, 4))
     dps = lax.axis_size("dp")
-    lrows = wl_hbm.shape[0]
+    yy = lax.rem(dp, 2)
+    zz = dp // 2
+    middle = (zz == 1) | (zz == 2)
+    zm = jnp.where(zz >= 2, 1, 0)
+    mate_y = (dp + 1 - 2 * yy, mp)
+    mate_e = ((zz + 1 - 2 * lax.rem(zz, 2)) * 2 + yy, mp)
+    mate_m = ((3 - zz) * 2 + yy, mp)
+    total = images * PAD
+    pairs = 24
+    kept = 8 * PAIR_IN
+    rs = big.at[pl.ds(0, total)]
+    gs = recv.at[pl.ds(kept, total)]
+    wup = recv.at[pl.ds(kept + total, width)]
+    wdn = recv.at[pl.ds(kept + total + width, width)]
 
     barrier = pltpu.get_barrier_semaphore()
     for device in (mate, across):
@@ -384,7 +400,7 @@
 
     def copy_x(i, par):
         return pltpu.make_async_remote_copy(
-            src_ref=tbuf.at[rows_of(i)], dst_ref=rx.at[par, rows_of(i)],
+            src_ref=pbuf.at[core, rows_of(i)], dst_ref=rx.at[par, rows_of(i)],
             send_sem=s_x.at[i], recv_sem=r_x.at[par, i], device_id=across, device_id_type=MESH,
         )
 
@@ -397,13 +413,13 @@
     def hop_two(i, par):
         copy_core(i).wait()
         rows = rows_of(i)
-        tbuf[rows] = (pbuf[core, rows].astype(f32) + rcore[rows].astype(f32)).astype(bf16)
+        pbuf[core, rows] = (pbuf[core, rows].astype(f32) + rcore[rows].astype(f32)).astype(bf16)
         copy_x(i, par).start()
 
     def hop_three(i, par):
         copy_x(i, par).wait()
         rows = rows_of(i)
-        sumb[core, rows] = (tbuf[rows].astype(f32) + rx[par, rows].astype(f32)).astype(bf16)
+        sumb[core, rows] = (pbuf[core, rows].astype(f32) + rx[par, rows].astype(f32)).astype(bf16)
         copy_ag(i).start()
 
     def arrived(i):
@@ -435,6 +451,158 @@
             hop_three(0, 1 - par)
         lax.fori_loop(0, images, step, 0)
         hop_two(images - 1, par)
+
+    def g_rows(k, lo, n):
+        return pl.ds(pl.multiple_of(lax.rem(k * 128 + 2048, 3072) + lo, 16), n)
+
+    def in_rows(k, lo, n):
+        return pl.ds(pl.multiple_of(k * PAIR_IN + lo, 16), n)
+
+    def send(k, slot, src, dst, device):
+        return pltpu.make_async_remote_copy(
+            src_ref=src, dst_ref=dst, send_sem=s_pair.at[slot, k], recv_sem=r_pair.at[slot, k],
+            device_id=device, device_id_type=MESH,
+        )
+
+    def y_swap(k):
+        return send(k, 0, big.at[g_rows(k, 32 - 32 * yy, 32)], recv.at[in_rows(k, 0, 32)], mate_y)
+
+    def y_end(k):
+        return send(k, 1, big.at[g_rows(k, 32 * yy, 32)], recv.at[in_rows(k, 32, 32)], mate_e)
+
+    def y_mid(k):
+        return send(k, 2, big.at[g_rows(k, 32 * yy, 32)], recv.at[in_rows(k, 64, 32)], mate_m)
+
+    def o_rows(k, lo, n):
+        return gall_hbm.at[pl.ds(pl.multiple_of(k * 128 + lo, 16), n)]
+
+    def y_back(k):
+        return send(k, 3, big.at[g_rows(k, 32 * yy, 32)], o_rows(k, 32 * yy, 32), mate_e)
+
+    def y_share_mid(k):
+        return send(k, 4, big.at[g_rows(k, 32 * yy, 32)], o_rows(k, 32 * yy, 32), mate_y)
+
+    def y_share_end(k):
+        return send(k, 4, o_rows(k, 32 * yy, 32), o_rows(k, 32 * yy, 32), mate_y)
+
+    def z_end(k):
+        return send(k, 5, big.at[g_rows(k, 64, 64)], recv.at[in_rows(k, 160, 64)], mate_e)
+
+    def z_mid(k):
+        return send(k, 6, big.at[g_rows(k, 96 - 32 * zm, 32)], recv.at[in_rows(k, 96, 32)], mate_m)
+
+    def z_swap(k):
+        return send(k, 7, big.at[g_rows(k, 64 + 32 * zm, 32)], recv.at[in_rows(k, 128, 32)], mate_y)
+
+    def z_share(k):
+        return send(k, 8, big.at[g_rows(k, 64 + 32 * zm, 32)], o_rows(k, 64 + 32 * zm, 32), mate_m)
+
+    def z_back(k):
+        return send(k, 9, big.at[g_rows(k, 64 + 32 * zm, 32)], o_rows(k, 64 + 32 * zm, 32), mate_e)
+
+    def z_pass(k):
+        return send(k, 10, o_rows(k, 96 - 32 * zm, 32), o_rows(k, 96 - 32 * zm, 32), mate_e)
+
+    def accumulate(k, lo, n, at):
+        rows = g_rows(k, lo, n)
+        big[rows, :] = (big[rows, :].astype(f32) + recv[in_rows(k, at, n), :].astype(f32)).astype(bf16)
+
+    def keep_y(k):
+        return pltpu.make_async_copy(big.at[g_rows(k, 32 * yy, 32)], o_rows(k, 32 * yy, 32), s_out.at[0, k])
+
+    def keep_z(k):
+        return pltpu.make_async_copy(
+            big.at[g_rows(k, 64 + 32 * zm, 32)], o_rows(k, 64 + 32 * zm, 32), s_out.at[1, k]
+        )
+
+    def hop0(k):
+        y_swap(k).start()
+
+        @pl.when(jnp.logical_not(middle))
+        def _():
+            z_end(k).start()
+
+    def hop1(k):
+        y_swap(k).wait()
+        accumulate(k, 32 * yy, 32, 0)
+
+        @pl.when(middle)
+        def _():
+            z_end(k).wait_recv()
+            accumulate(k, 64, 64, 160)
+            z_mid(k).start()
+
+        @pl.when(jnp.logical_not(middle))
+        def _():
+            y_end(k).start()
+
+    def hop2(k):
+        @pl.when(middle)
+        def _():
+            y_end(k).wait_recv()
+            accumulate(k, 32 * yy, 32, 32)
+            y_mid(k).start()
+            z_mid(k).wait()
+            accumulate(k, 64 + 32 * zm, 32, 96)
+            z_swap(k).start()
+
+    def hop3(k):
+        @pl.when(middle)
+        def _():
+            y_mid(k).wait()
+            accumulate(k, 32 * yy, 32, 64)
+            y_back(k).start()
+            y_share_mid(k).start()
+            keep_y(k).start()
+            z_swap(k).wait()
+            accumulate(k, 64 + 32 * zm, 32, 128)
+            z_share(k).start()
+            z_back(k).start()
+            keep_z(k).start()
+
+    def hop4(k):
+        @pl.when(middle)
+        def _():
+            z_share(k).wait()
+            z_pass(k).start()
+
+        @pl.when(jnp.logical_not(middle))
+        def _():
+            y_end(k).wait_send()
+            y_back(k).wait_recv()
+            y_share_end(k).start()
+
+    def hop5(k):
+        @pl.when(middle)
+        def _():
+            y_share_mid(k).wait()
+            y_back(k).wait_send()
+            z_back(k).wait_send()
+            z_pass(k).wait_send()
+            keep_y(k).wait()
+            keep_z(k).wait()
+
+        @pl.when(jnp.logical_not(middle))
+        def _():
+            y_share_end(k).wait()
+            z_end(k).wait_send()
+            z_back(k).wait_recv()
+            z_pass(k).wait_recv()
+
+    def tick(t):
+        for h, hop in ((5, hop5), (4, hop4), (3, hop3), (2, hop2), (1, hop1), (0, hop0)):
+            k = t - LAG * h
+
+            @pl.when((k >= 0) & (k < pairs))
+            def _(hop=hop, k=k):
+                hop(k)
+
+    def ticks(lo, hi):
+        def step(t, carry):
+            tick(t)
+            return carry
+
+        lax.fori_loop(lo, hi, step, 0)
 
     for k in (0, 1, 2, 3, 7):
         loads[k].wait()
@@ -499,9 +667,9 @@
 
     for k in range(1, dps):
         learn_copy(k).wait()
-    dg_ref[...] = jnp.zeros_like(dg_ref)
-    gl_ref[...] = jnp.zeros_like(gl_ref)
-    gsel_ref[...] = jnp.zeros_like(gsel_ref)
+    dg[...] = jnp.zeros_like(dg)
+    gl_sum[...] = jnp.zeros_like(gl_sum)
+    gsel_sum[...] = jnp.zeros_like(gsel_sum)
 
     def y_out(i):
         return pltpu.make_async_copy(d1s.at[rows_of(i)], y_hbm.at[rows_of(i)], sy.at[i])
@@ -532,14 +700,14 @@
         learned_ref[i] = tn(mb, y).astype(bf16)
         dmaps = nt(y, ct)
         dlog = (maps * (dmaps - jnp.sum(maps * dmaps, axis=0, keepdims=True))).astype(bf16)
-        gsel_ref[...] += tn(t, dlog)
+        gsel_sum[...] += tn(dlog, t)
         dzl = (nt(dlog, wsel) * slope).astype(bf16)
-        gl_ref[...] += tn(a3, dzl)
+        gl_sum[...] += tn(a3, dzl)
         for r in chunks():
             da3 = nt(dzl[r : r + CH], wlf)
             dy = nn(mb[r : r + CH], ct)
             u, s = stats(d1s[chunk_of(i, r), :].astype(f32))
-            dg_ref[2] += fold(da3 * u)
+            dg[2] += fold(da3 * u)
             dhs[chunk_of(i, r), :] = (dy + back(da3 * g3, u, s)).astype(bf16)
         dhb = dhs[rows, :]
         for c in range(4):
@@ -552,36 +720,31 @@
 
     stage(learner, 0)
 
-    def grad(left, right, ntile, out, col0, slot0):
-        wide = right.shape[1]
-
-        def g_out(j, slot):
-            return pltpu.make_async_copy(
-                gst.at[slot, :, pl.ds(0, wide)], out.at[pl.ds(pl.multiple_of(j * TILE, 16), TILE)], sg.at[slot]
-            )
-
+    def grad(left, right, first, tick0):
         def step(j, carry):
-            slot = lax.rem(j, 2)
-
-            @pl.when(j >= 2)
-            def _():
-                g_out(j - 2, slot).wait()
-
             lhs = left[:, pl.ds(pl.multiple_of(j * TILE, TILE), TILE)]
-            for c in range(0, wide, TILE):
-                gst[slot, :, c : c + TILE] = tn(lhs, right[:, c : c + TILE]).astype(bf16)
-            g_out(j, slot).start()
+            rows = g_rows(2 * (first + j), 0, TILE)
+            for c in range(0, width, TILE):
+                big[rows, c : c + TILE] = tn(lhs, right[:, c : c + TILE]).astype(bf16)
+            if tick0 is not None:
+                tick(tick0 + j)
             return carry
 
-        lax.fori_loop(0, ntile, step, 0)
-        for j in range(max(ntile - 2, 0), ntile):
-            g_out(j, j % 2).wait()
-
-    grad(rs, dhs, 4, gdn_hbm, 0, 0)
-    grad(a2s, gs, 4, gup_hbm, 0, 0)
+        lax.fori_loop(0, left.shape[1] // TILE, step, 0)
+
+    grad(rs, dhs, 0, 0)
+    grad(a2s, gs, 4, 4)
+    pl.semaphore_signal(ready_y, inc=1, device_id=mate_y, device_id_type=MESH)
+
+    @pl.when(middle)
+    def _():
+        pl.semaphore_signal(ready_z, inc=1, device_id=mate_e, device_id_type=MESH)
+        pl.semaphore_signal(ready_z, inc=1, device_id=mate_m, device_id_type=MESH)
 
     for i in range(images):
         y_out(i).wait()
+    pl.semaphore_wait(ready_y, 1)
+    pl.semaphore_wait(ready_z, 1)
 
     def attention_back(i):
         rows = rows_of(i)
@@ -589,7 +752,7 @@
             where = chunk_of(i, r)
             da2 = summed(i, r)
             u, s = stats(h1s[where, :])
-            dg_ref[1] += fold(da2 * u)
+            dg[1] += fold(da2 * u)
             d1s[where, :] = (dhs[where, :].astype(f32) + back(da2 * g2, u, s)).astype(bf16)
             ux, _ = stats(xs[where, :].astype(f32))
             a2s[where, :] = (ux * g1).astype(bf16)
@@ -619,13 +782,24 @@
         dall = qkv[rows, :]
         for c in range(4):
             store_p(i, c, nt(dall, wqkv[c * TILE : (c + 1) * TILE, :]))
+        tick(8 + i)
 
     stage(attention_back, 1)
-    grad(os, d1s, 1, gout_hbm, 0, 0)
-    grad(a2s, qkv, 4, gqkv_hbm, 0, 0)
+    grad(os, d1s, 8, 16)
+
+    def grad_qkv(j, carry):
+        lhs = a2s[:, pl.ds(pl.multiple_of(j * TILE, TILE), TILE)]
+        for c in range(3):
+            rows = g_rows(18 + 2 * c, 0, TILE)
+            big[rows, pl.ds(pl.multiple_of(j * TILE, TILE), TILE)] = tn(
+                lhs, qkv[:, c * TILE : (c + 1) * TILE]
+            ).astype(bf16)
+        return carry
+
+    lax.fori_loop(0, 4, grad_qkv, 0)
 
     def gp_out(i):
-        return pltpu.make_async_copy(rs.at[rows_of(i)], gp_hbm.at[rows_of(i)], sy.at[i])
+        return pltpu.make_async_copy(dhs.at[rows_of(i)], gp_hbm.at[rows_of(i)], sy.at[i])
 
     def finish(i, carry):
         @pl.when(i + 1 < images)
@@ -636,13 +810,47 @@
             where = chunk_of(i, r)
             da1 = summed(i, r)
             u, s = stats(xs[where, :].astype(f32))
-            dg_ref[0] += fold(da1 * u)
-            rs[where, :] = (d1s[where, :].astype(f32) + back(da1 * g1, u, s)).astype(bf16)
+            dg[0] += fold(da1 * u)
+            dhs[where, :] = (d1s[where, :].astype(f32) + back(da1 * g1, u, s)).astype(bf16)
         gp_out(i).start()
+        tick(17 + i)
         return carry
 
     hop_three(0, 1)
     lax.fori_loop(0, images, finish, 0)
+
+    small_mine[0:8, :] = jnp.concatenate(
+        [jnp.sum(dg[n], axis=0, keepdims=True) for n in range(3)] + [jnp.zeros((5, width), f32)], axis=0
+    ).astype(bf16)
+    small_mine[8:16, 0:64] = gsel_sum[...].astype(bf16)
+    small_mine[8:16, 64:width] = jnp.zeros((8, width - 64), bf16)
+    gl_mine[...] = gl_sum[...].astype(bf16).reshape(gl_mine.shape)
+
+    def small_copy(k):
+        peer = lax.rem(dp + k, dps)
+        return (
+            pltpu.make_async_remote_copy(
+                src_ref=small_mine, dst_ref=small_in.at[k - 1], send_sem=s_small.at[0, k - 1],
+                recv_sem=r_small.at[0, k - 1], device_id=(peer, mp), device_id_type=MESH,
+            ),
+            pltpu.make_async_remote_copy(
+                src_ref=gl_mine.at[peer], dst_ref=gl_in.at[k - 1], send_sem=s_small.at[1, k - 1],
+                recv_sem=r_small.at[1, k - 1], device_id=(peer, mp), device_id_type=MESH,
+            ),
+        )
+
+    for k in range(1, dps):
+        for copy in small_copy(k):
+            copy.start()
+    ticks(25, pairs + 5 * LAG)
+    for k in range(1, dps):
+        for copy in small_copy(k):
+            copy.wait()
+    small_ref[...] = small_mine[...].astype(f32)
+    gl_ref[...] = gl_mine[dp].astype(f32)
+    for k in range(dps - 1):
+        small_ref[...] += small_in[k].astype(f32)
+        gl_ref[...] += gl_in[k].astype(f32)
     for i in range(images):
         gp_out(i).wait()
 
@@ -668,41 +876,42 @@
             sds((images, 8, width), bf16),
             sds((total, width), bf16),
             sds((total, width), bf16),
-            sds((width, hidden), bf16),
-            sds((hidden, width), bf16),
-            sds((256, width), bf16),
-            sds((width, 768), bf16),
-            sds((3, 8, width), f32),
-            sds((width, learn_cols), f32),
-            sds((learn_cols, 8), f32),
+            sds((3072, width), bf16),
+            sds((16, width), f32),
+            sds((learn_rows, learn_cols), f32),
         ),
         in_specs=[anywhere] * 8 + [vmem] * 3 + [anywhere] + [vmem] * 2,
-        out_specs=(vmem,) + (anywhere,) * 6 + (vmem,) * 3,
+        out_specs=(vmem,) + (anywhere,) * 3 + (vmem,) * 2,
         scratch_shapes=[
             pltpu.VMEM((2, count, width), bf16),
             pltpu.VMEM((images, 1, PAD), f32),
             pltpu.VMEM((width, 768), bf16),
             pltpu.VMEM((256, width), bf16),
-            pltpu.VMEM((width, hidden), bf16),
-            pltpu.VMEM((hidden, width), bf16),
             pltpu.VMEM((dps, learn_rows, learn_cols), bf16),
             pltpu.VMEM((total, width), bf16),
             pltpu.VMEM((total, 768), bf16),
             pltpu.VMEM((total, 256), bf16),
             pltpu.VMEM((total, width), f32),
             pltpu.VMEM((total, width), bf16),
-            pltpu.VMEM((total, hidden), bf16),
-            pltpu.VMEM((total, hidden), bf16),
             pltpu.VMEM((total, width), bf16),
             pltpu.VMEM((total, width), bf16),
+            pltpu.VMEM((3072, width), bf16),
+            pltpu.VMEM((8 * PAIR_IN + total + 2 * width, width), bf16),
             pltpu.VMEM((2, total, width // 2), bf16),
-            pltpu.VMEM((total, width // 2), bf16),
             pltpu.VMEM((total, width // 2), bf16),
             pltpu.VMEM((2, total, width // 2), bf16),
             pltpu.VMEM((2, total, width // 2), bf16),
-            pltpu.VMEM((2, TILE, width), bf16),
-            dma((2,)), dma((8,)), dma((images,)), dma((2,)), dma((dps - 1,)), dma((dps - 1,)),
+            pltpu.VMEM((3, 8, width), f32),
+            pltpu.VMEM((width, learn_cols), f32),
+            pltpu.VMEM((8, learn_cols), f32),
+            pltpu.VMEM((dps, learn_rows, learn_cols), bf16),
+            pltpu.VMEM((dps - 1, learn_rows, learn_cols), bf16),
+            pltpu.VMEM((16, width), bf16),
+            pltpu.VMEM((dps - 1, 16, width), bf16),
+            dma((2,)), dma((8,)), dma((images,)), dma((dps - 1,)), dma((dps - 1,)),
             dma((images,)), dma((images,)), dma((images,)), dma((2, images)), dma((images,)), dma((images,)),
+            dma((11, 24)), dma((11, 24)), dma((2, 24)),
+            pltpu.SemaphoreType.REGULAR, pltpu.SemaphoreType.REGULAR, dma((2, dps - 1)), dma((2, dps - 1)),
         ],
         compiler_params=pltpu.CompilerParams(
             collective_id=0, has_side_effects=True, vmem_limit_bytes=60 * 2**20
@@ -711,20 +920,18 @@
         patches, bias, w_query, w_key, w_value, w_out, w_up, w_down,
         gain_attn[None], gain_mlp[None], gain_learn[None], w_learn, w_select, cotangent,
     )
-    learned, y, gpat, gup, gdn, gout, gqkv, dg, gl, gsel = outs
+    learned, y, gpat, gall, small, gl = outs
     y = y.reshape(images, PAD, width)[:, :count]
     gpat = gpat.reshape(images, PAD, width)[:, :count]
 
-    def over_dp(v):
-        return lax.psum(v.astype(bf16), "dp").astype(f32)
-
-    gup, gdn, gout, gqkv = over_dp(gup), over_dp(gdn), over_dp(gout), over_dp(gqkv)
-    dg = over_dp(jnp.sum(dg, axis=1))
-    gl, gsel = over_dp(gl), over_dp(gsel)
-    gl = lax.dynamic_slice_in_dim(gl, lax.axis_index("dp") * learn_rows, learn_rows, 0)
+    def stacked(first):
+        v = gall[first : first + 256].reshape(256, 4, 256).astype(f32)
+        return v.transpose(1, 0, 2).reshape(width, 256)
+
     return (
-        learned, y, gpat, gqkv[:, :256], gqkv[:, 256:512], gqkv[:, 512:], gout, gup, gdn,
-        dg[0], dg[1], dg[2], gl, gsel,
+        learned, y, gpat, stacked(2304), stacked(2560), stacked(2816), gall[2048:2304].astype(f32),
+        gall[1024:2048].astype(f32), gall[0:1024].astype(f32),
+        small[0], small[1], small[2], gl, small[8:16, :learn_cols].T,
     )
 
 

time: 422 us -> 291 us (0.69)
  waiting for transfers between devices: 173 us -> 0 us
  Pallas kernels: 163 us -> 250 us
  blocking collectives: 36.9 us -> 0 us
  between operations: 14.1 us -> 0.7 us
  local copies, waits for them, and re-layouts: 23.7 us -> 28.6 us
    psum x1 -> x0, waiting for transfers between devices: 173 us -> none  [over_dp(): return lax.psum(v.astype(bf16), 'dp').astype(f32)]
    pallas_call x1, Pallas kernels: 163 us -> 250 us  [local_fused(): pl.pallas_call(fused, name='block', out_shape=(sds((images, 8, width), bf...]
    psum x1 -> x0, blocking collectives: 36.9 us -> none  [over_dp(): return lax.psum(v.astype(bf16), 'dp').astype(f32)]
    reshape x0 -> x6, local copies, waits for them, and re-layouts: none -> 6.17 us  [stacked(): return v.transpose(1, 0, 2).reshape(width, 256)]
    unnamed x24 -> x13, local copies, waits for them, and re-layouts: 20.1 us -> 16.5 us
    convert_element_type x6 -> x2, other arithmetic: 9.74 us -> 9.99 us  [the longest x1 6.7 us: local_fused(): gall[0:1024].astype(f32)]
  transfers between devices with their start and end apart: 1 -> 0, of which waited for: 1 -> 0; matrix products, arithmetic and copies ran while one was open for 2% -> 0% of each run, Pallas kernels for 0% -> 0%
where the time goes in v2:
time: 291 us; the launch traced here: 290 us
  Pallas kernels  250 us (86%)
  local copies, waits for them, and re-layouts  28.6 us (10%)
  other arithmetic  10.7 us (4%)
    pallas_call x1, Pallas kernels, local_fused(): pl.pallas_call(fused, name='block', out_shape=(sds((images, 8, width), bf...  250 us
    unnamed x13, local copies, waits for them, and re-layouts  16.5 us
    convert_element_type x1, other arithmetic, local_fused(): gall[0:1024].astype(f32)  6.7 us
    reshape x6, local copies, waits for them, and re-layouts, stacked(): return v.transpose(1, 0, 2).reshape(width, 256)  6.17 us

profile of v2, /device:TPU:0, one launch (start us, length us, event | category | flops | bytes accessed | tf_op | source)
XLA Modules:
  0.0 290.1 jit_solution(15102527524688911690)
XLA Ops:
  0.6 0.7 fusion
  1.3 0.6 broadcast_in_dim.22.bias_hbm
  2.0 1.4 copy.30.wsel_ref
  3.3 1.4 copy.29.wl_hbm
  4.8 5.4 %copy.28.patches = bf16[8,196,1024]{2,1,0:T(8,128)(2,1)} copy(bf16[8,196,1024]{2,0,1:T(8,128)(2,1)} %param.14) | data formatting | bytes 6422528 | tf_op args[0]
  10.1 250.1 %block.1 = (bf16[8,8,1024]{2,1,0:T(8,128)(2,1)}, bf16[1664,1024]{1,0:T(8,128)(2,1)}, bf16[1664,1024]{1,0:T(8,128)(2,1)}, bf16[3072,1024]{1,0:T(8,128)(2,1)}, f32[16,1024]{1,0:T(8,128)}, /*index=5*/f32[128,64]{1,0:T(8,128)}) custom-call(bf16[8,196,1024]{2,1,0:T(8,128)(2,1)} %copy.28.patches, f32[8,1,208]{2,1,0:T(1,128)} %broadcast_in_dim.22.bias_hbm, ...), custom_call_target="tpu_custom_call" | custom-call | tf_op jit(solution)/shard_map/block/pallas_call | solution.py:872
  260.2 2.3 slice.48
  262.5 0.0 copy-start.2
  262.5 0.0 copy-start
  262.5 3.5 %copy.37 = bf16[8,196,1024]{2,0,1:T(8,128)(2,1)} copy(bf16[8,196,1024]{2,1,0:T(8,128)(2,1)S(1)} %slice.48) | data formatting | bytes 6422528
  265.9 1.3 slice_bitcast_fusion
  267.2 1.5 fusion.1
  268.7 0.0 copy-done.2
  268.7 0.7 copy.36
  269.4 0.0 copy-done
  269.4 0.4 slice.49
  269.8 3.5 %copy.38 = bf16[8,196,1024]{2,0,1:T(8,128)(2,1)} copy(bf16[8,196,1024]{2,1,0:T(8,128)(2,1)S(1)} %slice.49) | data formatting | bytes 6422528
  273.2 3.3 %slice_convert_fusion.2 = (f32[256,1024]{1,0:T(8,128)}, f32[256,1024]{1,0:T(8,128)}, f32[256,1024]{1,0:T(8,128)S(1)}, f32[256,1024]{1,0:T(8,128)S(1)}) fusion(bf16[3072,1024]{1,0:T(8,128)(2,1)} %get-tuple-element.23), kind=kLoop, calls=%fused_computation.2 | loop fusion | flops 1048576 | bytes 6291456 | tf_op jit(solution)/shard_map/convert_element_type | solution.py:932
  276.5 1.7 reshape.83
  278.2 1.2 copy.35
  279.4 0.5 reshape.81
  279.9 1.2 copy.34
  281.0 0.5 reshape.79
  281.5 1.2 copy.33
  282.7 0.0 copy-start.1
  282.7 6.7 %slice_convert_fusion = (f32[1024,1024]{1,0:T(8,128)}, f32[1024,1024]{1,0:T(8,128)}) fusion(bf16[3072,1024]{1,0:T(8,128)(2,1)} %get-tuple-element.23), kind=kLoop, calls=%fused_computation | loop fusion | flops 2097152 | bytes 12582912 | tf_op jit(solution)/shard_map/convert_element_type | solution.py:933
  289.4 0.0 copy-done.1
  289.4 0.7 copy.40
Async XLA Ops:
  262.5 6.2 %copy-start.2 = (f32[128,64]{1,0:T(8,128)S(1)}, f32[128,64]{1,0:T(8,128)}, u32[]{:S(2)}) copy-start(f32[128,64]{1,0:T(8,128)} %get-tuple-element.38) | copy-start | bytes 98308
  262.5 6.9 %copy-start = (bf16[1664,1024]{1,0:T(8,128)(2,1)S(1)}, bf16[1664,1024]{1,0:T(8,128)(2,1)}, u32[]{:S(2)}) copy-start(bf16[1664,1024]{1,0:T(8,128)(2,1)} %get-tuple-element.22) | copy-start | bytes 10223620
  282.7 6.7 %copy-start.1 = (bf16[8,8,1024]{2,1,0:T(8,128)(2,1)S(1)}, bf16[8,8,1024]{2,1,0:T(8,128)(2,1)}, u32[]{:S(2)}) copy-start(bf16[8,8,1024]{2,1,0:T(8,128)(2,1)} %get-tuple-element.63) | copy-start | bytes 393220

commit v3 on v2

--- a/solution.py
+++ b/solution.py
@@ -302,18 +302,17 @@
 
 
 def fused(
-    patches, bias_hbm, wq_hbm, wk_hbm, wv_hbm, wo_hbm, wup_hbm, wdn_hbm, g1_ref, g2_ref, g3_ref,
+    patches, keep_ref, wq_hbm, wk_hbm, wv_hbm, wo_hbm, wup_hbm, wdn_hbm, g1_ref, g2_ref, g3_ref,
     wl_hbm, wsel_ref, ct_ref,
     learned_ref, y_hbm, gp_hbm, gall_hbm, small_ref, gl_ref,
-    xraw, bias, wqkv, wo, wl,
+    bias, wqkv, wo, wl,
     xs, qkv, os, h1s, a2s, dhs, d1s, big, recv,
     pbuf, rcore, rx, sumb, dg, gl_sum, gsel_sum, gl_mine, gl_in, small_mine, small_in,
     sx, sw, sy, slearn_s, slearn_r, s_core, r_core, s_x, r_x, s_ag, r_ag,
     s_pair, r_pair, s_out, ready_y, ready_z, s_small, r_small,
 ):
-    images = patches.shape[0]
-    count = patches.shape[1]
-    width = patches.shape[2]
+    images, count = keep_ref.shape
+    width = patches.shape[1]
     half = width // 2
     dp = lax.axis_index("dp")
     mp = lax.axis_index("mp")
@@ -332,15 +331,18 @@
     pairs = 24
     kept = 8 * PAIR_IN
     rs = big.at[pl.ds(0, total)]
-    gs = recv.at[pl.ds(kept, total)]
-    wup = recv.at[pl.ds(kept + total, width)]
-    wdn = recv.at[pl.ds(kept + total + width, width)]
+    wup = recv.at[pl.ds(kept, width)]
+    wdn = recv.at[pl.ds(kept + width, width)]
+    gs = recv.at[pl.ds(kept + 2 * width, total)]
 
     barrier = pltpu.get_barrier_semaphore()
     for device in (mate, across):
         pl.semaphore_signal(barrier, inc=1, device_id=device, device_id_type=MESH)
     for k in range(1, dps):
         pl.semaphore_signal(barrier, inc=1, device_id=(lax.rem(dp + k, dps), mp), device_id_type=MESH)
+
+    def wl_part(d):
+        return wl.at[:, pl.ds(pl.multiple_of(d * wl_hbm.shape[1], 128), wl_hbm.shape[1])]
 
     loads = [
         pltpu.make_async_copy(wq_hbm, wqkv.at[:, pl.ds(0, 256)], sw.at[0]),
@@ -349,27 +351,24 @@
         pltpu.make_async_copy(wo_hbm, wo, sw.at[3]),
         pltpu.make_async_copy(wup_hbm, wup, sw.at[4]),
         pltpu.make_async_copy(wdn_hbm, wdn, sw.at[5]),
-        pltpu.make_async_copy(wl_hbm, wl.at[dp], sw.at[6]),
-        pltpu.make_async_copy(bias_hbm, bias, sw.at[7]),
+        pltpu.make_async_copy(wl_hbm, wl_part(dp), sw.at[6]),
     ]
 
-    def load_x(i, slot):
-        return pltpu.make_async_copy(patches.at[i], xraw.at[slot], sx.at[slot])
-
-    load_x(0, 0).start()
-    for k in (0, 1, 2, 7, 3):
+    load_x = pltpu.make_async_copy(patches, dhs.at[pl.ds(0, images * count)], sx)
+    load_x.start()
+    for k in (0, 1, 2, 3, 6, 4, 5):
         loads[k].start()
-    load_x(1, 1).start()
-    for k in (6, 4, 5):
-        loads[k].start()
 
     xs[...] = jnp.zeros_like(xs)
+    bias[...] = jnp.full(bias.shape, -1e30, f32)
+    for i in range(images):
+        bias[i, :, 0:count] = jnp.where(keep_ref[i : i + 1, :] > 0, 0.0, -1e30)
 
     pl.semaphore_wait(barrier, dps + 1)
 
     def learn_copy(k):
         return pltpu.make_async_remote_copy(
-            src_ref=wl.at[dp], dst_ref=wl.at[dp],
+            src_ref=wl_part(dp), dst_ref=wl_part(dp),
             send_sem=slearn_s.at[k - 1], recv_sem=slearn_r.at[k - 1],
             device_id=(lax.rem(dp + k, dps), mp), device_id_type=MESH,
         )
@@ -385,6 +384,13 @@
 
     def only(v, h):
         return jnp.where(lane_head == h, v, jnp.zeros_like(v))
+
+    def put_wide(where, value):
+        for c in range(width // 128):
+            h1s[c, where, :] = value[:, c * 128 : (c + 1) * 128]
+
+    def get_wide(where):
+        return jnp.concatenate([h1s[c, where, :] for c in range(width // 128)], axis=1)
 
     def rows_of(i):
         return pl.ds(pl.multiple_of(i * PAD, 16), PAD)
@@ -432,25 +438,40 @@
     def store_p(i, t, value):
         pbuf[t // 2, rows_of(i), (t % 2) * TILE : (t % 2 + 1) * TILE] = value.astype(bf16)
 
-    def stage(body, par, first=False):
+    def stage(body, lo, hi, second, before=None):
         def step(i, carry):
-            if not first:
-                @pl.when(i + 1 < images)
-                def _():
-                    hop_three(i + 1, 1 - par)
-                arrived(i)
+            if before is not None:
+                before(i, hi)
             body(i)
             copy_core(i).start()
 
-            @pl.when(i > 0)
+            @pl.when(i > lo)
             def _():
-                hop_two(i - 1, par)
+                second(i - 1)
             return carry
 
-        if not first:
-            hop_three(0, 1 - par)
-        lax.fori_loop(0, images, step, 0)
-        hop_two(images - 1, par)
+        lax.fori_loop(lo, hi, step, 0)
+        second(hi - 1)
+
+    def far(par):
+        return lambda i: hop_two(i, par)
+
+    def from_far(par):
+        def before(i, hi):
+            @pl.when(i + 1 < hi)
+            def _():
+                hop_three(i + 1, par)
+            arrived(i)
+        return before
+
+    def each(body, lo, hi, before=None):
+        def step(i, carry):
+            if before is not None:
+                before(i, hi)
+            body(i)
+            return carry
+
+        lax.fori_loop(lo, hi, step, 0)
 
     def g_rows(k, lo, n):
         return pl.ds(pl.multiple_of(lax.rem(k * 128 + 2048, 3072) + lo, 16), n)
@@ -604,19 +625,26 @@
 
         lax.fori_loop(lo, hi, step, 0)
 
-    for k in (0, 1, 2, 3, 7):
+    load_x.wait()
+    for r in range(0, images * count, 8 * CH):
+        top = min(r + 8 * CH, images * count)
+        put_wide(pl.ds(r, top - r), dhs[r:top, :].astype(f32))
+    for k in (0, 1, 2, 3):
         loads[k].wait()
 
+    def attend(q, k, v, row_bias):
+        o = jnp.zeros((PAD, 256), f32)
+        for h in range(4):
+            scores = nt(only(q, h), k) + row_bias
+            e = jnp.exp(scores - jnp.max(scores, axis=1, keepdims=True))
+            p = (e * (1.0 / jnp.sum(e, axis=1, keepdims=True))).astype(bf16)
+            o = o + nn(p, only(v, h))
+        return o.astype(bf16)
+
     def attention(i):
-        slot = lax.rem(i, 2)
-        load_x(i, slot).wait()
         start = pl.multiple_of(i * PAD, 16)
-        xs[pl.ds(start, count), :] = xraw[slot]
-
-        @pl.when(i + 2 < images)
-        def _():
-            load_x(i + 2, slot).start()
-
+        for c in range(width // 128):
+            xs[pl.ds(start, count), c * 128 : (c + 1) * 128] = h1s[c, pl.ds(i, count, stride=images), :].astype(bf16)
         for r in chunks():
             u, _ = stats(xs[chunk_of(i, r), :].astype(f32))
             a2s[chunk_of(i, r), :] = (u * g1).astype(bf16)
@@ -625,22 +653,15 @@
         qkv[rows, 0:256] = (nn(a1, wqkv[:, 0:256]) * 0.125).astype(bf16)
         qkv[rows, 256:512] = nn(a1, wqkv[:, 256:512]).astype(bf16)
         qkv[rows, 512:768] = nn(a1, wqkv[:, 512:768]).astype(bf16)
-        q = qkv[rows, 0:256]
-        k = qkv[rows, 256:512]
-        v = qkv[rows, 512:768]
-        row_bias = bias[i]
-        o = jnp.zeros((PAD, 256), f32)
-        for h in range(4):
-            scores = nt(only(q, h), k) + row_bias
-            e = jnp.exp(scores - jnp.max(scores, axis=1, keepdims=True))
-            p = (e * (1.0 / jnp.sum(e, axis=1, keepdims=True))).astype(bf16)
-            o = o + nn(p, only(v, h))
-        ob = o.astype(bf16)
-        os[rows, :] = ob
+        os[rows, :] = attend(qkv[rows, 0:256], qkv[rows, 256:512], qkv[rows, 512:768], bias[i])
+
+    def attention_sent(i):
+        attention(i)
+        ob = os[rows_of(i), :]
         for t in range(4):
             store_p(i, t, nn(ob, wo[:, t * TILE : (t + 1) * TILE]))
 
-    stage(attention, 0, first=True)
+    stage(attention_sent, 0, images, far(0))
 
     loads[4].wait()
     loads[5].wait()
@@ -648,7 +669,7 @@
     def mlp(i):
         for r in chunks():
             h1 = xs[chunk_of(i, r), :].astype(f32) + summed(i, r)
-            h1s[chunk_of(i, r), :] = h1
+            put_wide(chunk_of(i, r), h1)
             u, _ = stats(h1)
             a2s[chunk_of(i, r), :] = (u * g2).astype(bf16)
         rows = rows_of(i)
@@ -663,7 +684,8 @@
         for t in range(4):
             store_p(i, t, nn(act, wdn[:, t * TILE : (t + 1) * TILE]))
 
-    stage(mlp, 1)
+    hop_three(0, 0)
+    stage(mlp, 0, images, far(1), from_far(0))
 
     for k in range(1, dps):
         learn_copy(k).wait()
@@ -677,23 +699,23 @@
     def learner(i):
         rows = rows_of(i)
         for r in chunks():
-            yb = (h1s[chunk_of(i, r), :] + summed(i, r)).astype(bf16)
+            yb = (get_wide(chunk_of(i, r)) + summed(i, r)).astype(bf16)
             d1s[chunk_of(i, r), :] = yb
             u, _ = stats(yb.astype(f32))
             dhs[chunk_of(i, r), :] = (u * g3).astype(bf16)
         y_out(i).start()
         y = d1s[rows, :]
         a3 = dhs[rows, :]
-        wlf = wl[...].reshape(width, wl.shape[2])
+        wlf = wl[...]
         wsel = wsel_ref[...]
         ct = ct_ref[i]
-        zl = nn(a3, wlf)
+        zl = nt(a3, wlf)
         cdf, pdf = gauss(zl)
         t = (zl * cdf).astype(bf16)
         slope = cdf + zl * pdf
         eye = lax.broadcasted_iota(jnp.int32, (PAD, PAD), 0) == lax.broadcasted_iota(jnp.int32, (PAD, PAD), 1)
         col_bias = jnp.sum(jnp.where(eye, bias[i], 0.0), axis=1, keepdims=True)
-        logits = nn(t, wsel) + col_bias
+        logits = nt(t, wsel) + col_bias
         e = jnp.exp(logits - jnp.max(logits, axis=0, keepdims=True))
         maps = e * (1.0 / jnp.sum(e, axis=0, keepdims=True))
         mb = maps.astype(bf16)
@@ -701,14 +723,17 @@
         dmaps = nt(y, ct)
         dlog = (maps * (dmaps - jnp.sum(maps * dmaps, axis=0, keepdims=True))).astype(bf16)
         gsel_sum[...] += tn(dlog, t)
-        dzl = (nt(dlog, wsel) * slope).astype(bf16)
-        gl_sum[...] += tn(a3, dzl)
+        dzl = (nn(dlog, wsel) * slope).astype(bf16)
+        gl_sum[...] += tn(dzl, a3)
         for r in chunks():
-            da3 = nt(dzl[r : r + CH], wlf)
+            da3 = nn(dzl[r : r + CH], wlf)
             dy = nn(mb[r : r + CH], ct)
             u, s = stats(d1s[chunk_of(i, r), :].astype(f32))
             dg[2] += fold(da3 * u)
             dhs[chunk_of(i, r), :] = (dy + back(da3 * g3, u, s)).astype(bf16)
+
+    def mlp_back(i):
+        rows = rows_of(i)
         dhb = dhs[rows, :]
         for c in range(4):
             cols = slice(c * TILE, (c + 1) * TILE)
@@ -718,7 +743,12 @@
         for c in range(4):
             store_p(i, c, nt(dz, wup[c * TILE : (c + 1) * TILE, :]))
 
-    stage(learner, 0)
+    def learner_mlp(i):
+        learner(i)
+        mlp_back(i)
+
+    hop_three(0, 1)
+    stage(learner_mlp, 0, images, far(0), from_far(1))
 
     def grad(left, right, first, tick0):
         def step(j, carry):
@@ -732,26 +762,30 @@
 
         lax.fori_loop(0, left.shape[1] // TILE, step, 0)
 
+    def ready():
+        pl.semaphore_signal(ready_y, inc=1, device_id=mate_y, device_id_type=MESH)
+
+        @pl.when(middle)
+        def _():
+            pl.semaphore_signal(ready_z, inc=1, device_id=mate_e, device_id_type=MESH)
+            pl.semaphore_signal(ready_z, inc=1, device_id=mate_m, device_id_type=MESH)
+
+    def both_ready():
+        pl.semaphore_wait(ready_y, 1)
+        pl.semaphore_wait(ready_z, 1)
+
     grad(rs, dhs, 0, 0)
     grad(a2s, gs, 4, 4)
-    pl.semaphore_signal(ready_y, inc=1, device_id=mate_y, device_id_type=MESH)
-
-    @pl.when(middle)
-    def _():
-        pl.semaphore_signal(ready_z, inc=1, device_id=mate_e, device_id_type=MESH)
-        pl.semaphore_signal(ready_z, inc=1, device_id=mate_m, device_id_type=MESH)
-
+    ready()
     for i in range(images):
         y_out(i).wait()
-    pl.semaphore_wait(ready_y, 1)
-    pl.semaphore_wait(ready_z, 1)
 
     def attention_back(i):
         rows = rows_of(i)
         for r in chunks():
             where = chunk_of(i, r)
             da2 = summed(i, r)
-            u, s = stats(h1s[where, :])
+            u, s = stats(get_wide(where))
             dg[1] += fold(da2 * u)
             d1s[where, :] = (dhs[where, :].astype(f32) + back(da2 * g2, u, s)).astype(bf16)
             ux, _ = stats(xs[where, :].astype(f32))
@@ -784,16 +818,19 @@
             store_p(i, c, nt(dall, wqkv[c * TILE : (c + 1) * TILE, :]))
         tick(8 + i)
 
-    stage(attention_back, 1)
+    hop_three(0, 0)
+    both_ready()
+    stage(attention_back, 0, images, far(1), from_far(0))
     grad(os, d1s, 8, 16)
 
     def grad_qkv(j, carry):
         lhs = a2s[:, pl.ds(pl.multiple_of(j * TILE, TILE), TILE)]
-        for c in range(3):
-            rows = g_rows(18 + 2 * c, 0, TILE)
-            big[rows, pl.ds(pl.multiple_of(j * TILE, TILE), TILE)] = tn(
-                lhs, qkv[:, c * TILE : (c + 1) * TILE]
-            ).astype(bf16)
+        for n in range(3):
+            value = tn(lhs, qkv[:, n * TILE : (n + 1) * TILE]).astype(bf16)
+            rows = pl.ds(pl.multiple_of(1280 + j * 192 + n * 64, 16), 64)
+            for c in range(4):
+                big[rows, c * TILE : (c + 1) * TILE] = value[c * 64 : (c + 1) * 64]
+        tick(17 + j)
         return carry
 
     lax.fori_loop(0, 4, grad_qkv, 0)
@@ -813,7 +850,7 @@
             dg[0] += fold(da1 * u)
             dhs[where, :] = (d1s[where, :].astype(f32) + back(da1 * g1, u, s)).astype(bf16)
         gp_out(i).start()
-        tick(17 + i)
+        tick(21 + i)
         return carry
 
     hop_three(0, 1)
@@ -824,7 +861,11 @@
     ).astype(bf16)
     small_mine[8:16, 0:64] = gsel_sum[...].astype(bf16)
     small_mine[8:16, 64:width] = jnp.zeros((8, width - 64), bf16)
-    gl_mine[...] = gl_sum[...].astype(bf16).reshape(gl_mine.shape)
+    gl_mine[...] = gl_sum[...].astype(bf16)
+    part = wl_hbm.shape[1]
+
+    def gl_part(d):
+        return pl.ds(pl.multiple_of(d * part, 128), part)
 
     def small_copy(k):
         peer = lax.rem(dp + k, dps)
@@ -834,7 +875,7 @@
                 recv_sem=r_small.at[0, k - 1], device_id=(peer, mp), device_id_type=MESH,
             ),
             pltpu.make_async_remote_copy(
-                src_ref=gl_mine.at[peer], dst_ref=gl_in.at[k - 1], send_sem=s_small.at[1, k - 1],
+                src_ref=gl_mine.at[:, gl_part(peer)], dst_ref=gl_in.at[k - 1], send_sem=s_small.at[1, k - 1],
                 recv_sem=r_small.at[1, k - 1], device_id=(peer, mp), device_id_type=MESH,
             ),
         )
@@ -842,17 +883,91 @@
     for k in range(1, dps):
         for copy in small_copy(k):
             copy.start()
-    ticks(25, pairs + 5 * LAG)
+    ticks(29, pairs + 5 * LAG)
     for k in range(1, dps):
         for copy in small_copy(k):
             copy.wait()
     small_ref[...] = small_mine[...].astype(f32)
-    gl_ref[...] = gl_mine[dp].astype(f32)
+    gl_ref[...] = gl_mine[:, gl_part(dp)].astype(f32)
     for k in range(dps - 1):
         small_ref[...] += small_in[k].astype(f32)
         gl_ref[...] += gl_in[k].astype(f32)
     for i in range(images):
         gp_out(i).wait()
+
+
+def finish_up(
+    gall, y, gp, learned, small, gl,
+    learned_ref, y_ref, gp_ref, gq_ref, gk_ref, gv_ref, gout_ref, gup_ref, gdn_ref, d1_ref, d2_ref, d3_ref,
+    gl_ref, gsel_ref,
+    tiles, y_in, gp_in, wide, square, y_turned, gp_turned, strip, s_tile, s_in, s_wide, s_square, s_turned,
+):
+    count = y_ref.shape[0]
+
+    def tile_in(j):
+        rows = pl.ds(j * TILE, TILE)
+        return pltpu.make_async_copy(gall.at[rows], tiles.at[rows], s_tile.at[j])
+
+    ins = [pltpu.make_async_copy(y, y_in, s_in.at[0]), pltpu.make_async_copy(gp, gp_in, s_in.at[1])]
+    for j in range(4):
+        tile_in(j).start()
+    for copy in ins:
+        copy.start()
+    for j in range(4, 12):
+        tile_in(j).start()
+    outs = []
+
+    def tile_out(j):
+        tile_in(j).wait()
+        rows = slice(j * TILE, (j + 1) * TILE)
+        wide[rows, :] = tiles[rows, :].astype(f32)
+        ref, first = ((gdn_ref, 0), (gup_ref, 4), (gout_ref, 8))[j // 4]
+        copy = pltpu.make_async_copy(
+            wide.at[pl.ds(j * TILE, TILE)], ref.at[pl.ds((j - first) * TILE, TILE)], s_wide.at[j]
+        )
+        copy.start()
+        outs.append(copy)
+
+    def turn(n, src, dst, ref):
+        ins[n].wait()
+        for block in range(0, count, CH):
+            rows = min(CH, count - block)
+            for c in range(src.shape[2] // 128):
+                cols = slice(c * 128, (c + 1) * 128)
+                slot = strip.at[c]
+                slot[...] = src[:, block : block + CH, cols].astype(f32).reshape(slot.shape)
+                for r in range(rows):
+                    dst[block + r, :, cols] = slot[pl.ds(r, dst.shape[1], stride=CH), :].astype(bf16)
+            copy = pltpu.make_async_copy(
+                dst.at[pl.ds(block, rows)], ref.at[pl.ds(block, rows)], s_turned.at[n, block // CH]
+            )
+            copy.start()
+            outs.append(copy)
+
+    for j in range(4):
+        tile_out(j)
+    turn(0, y_in, y_turned, y_ref)
+    for j in range(4, 9):
+        tile_out(j)
+    turn(1, gp_in, gp_turned, gp_ref)
+    for j in range(9, 12):
+        tile_in(j).wait()
+    for n, ref in enumerate((gq_ref, gk_ref, gv_ref)):
+        for j in range(4):
+            for c in range(4):
+                square[n, j * TILE + c * 64 : j * TILE + (c + 1) * 64, :] = tiles[
+                    9 * TILE + j * 192 + n * 64 : 9 * TILE + j * 192 + (n + 1) * 64, c * TILE : (c + 1) * TILE
+                ].astype(f32)
+        copy = pltpu.make_async_copy(square.at[n], ref, s_square.at[n])
+        copy.start()
+        outs.append(copy)
+    learned_ref[...] = learned[...]
+    for n, ref in enumerate((d1_ref, d2_ref, d3_ref)):
+        ref[...] = small[n : n + 1, :]
+    gl_ref[...] = gl[...]
+    gsel_ref[...] = small[8:16, 0 : gsel_ref.shape[1]]
+    for copy in outs:
+        copy.wait()
 
 
 def local_fused(
@@ -862,7 +977,6 @@
     images, count, width = patches.shape
     total = images * PAD
     hidden = w_up.shape[1]
-    bias = jnp.where(jnp.pad(keep_mask, ((0, 0), (0, PAD - count))) > 0, 0.0, -1e30).astype(f32)[:, None, :]
     learn_rows, learn_cols = w_learn.shape
     dps = lax.axis_size("dp")
     anywhere = pl.BlockSpec(memory_space=pl.ANY)
@@ -878,20 +992,19 @@
             sds((total, width), bf16),
             sds((3072, width), bf16),
             sds((16, width), f32),
-            sds((learn_rows, learn_cols), f32),
+            sds((learn_cols, learn_rows), f32),
         ),
-        in_specs=[anywhere] * 8 + [vmem] * 3 + [anywhere] + [vmem] * 2,
+        in_specs=[anywhere, vmem] + [anywhere] * 6 + [vmem] * 3 + [anywhere] + [vmem] * 2,
         out_specs=(vmem,) + (anywhere,) * 3 + (vmem,) * 2,
         scratch_shapes=[
-            pltpu.VMEM((2, count, width), bf16),
             pltpu.VMEM((images, 1, PAD), f32),
             pltpu.VMEM((width, 768), bf16),
             pltpu.VMEM((256, width), bf16),
-            pltpu.VMEM((dps, learn_rows, learn_cols), bf16),
+            pltpu.VMEM((learn_cols, width), bf16),
             pltpu.VMEM((total, width), bf16),
             pltpu.VMEM((total, 768), bf16),
             pltpu.VMEM((total, 256), bf16),
-            pltpu.VMEM((total, width), f32),
+            pltpu.VMEM((width // 128, total, 128), f32),
             pltpu.VMEM((total, width), bf16),
             pltpu.VMEM((total, width), bf16),
             pltpu.VMEM((total, width), bf16),
@@ -902,13 +1015,13 @@
             pltpu.VMEM((2, total, width // 2), bf16),
             pltpu.VMEM((2, total, width // 2), bf16),
             pltpu.VMEM((3, 8, width), f32),
-            pltpu.VMEM((width, learn_cols), f32),
+            pltpu.VMEM((learn_cols, width), f32),
             pltpu.VMEM((8, learn_cols), f32),
-            pltpu.VMEM((dps, learn_rows, learn_cols), bf16),
-            pltpu.VMEM((dps - 1, learn_rows, learn_cols), bf16),
+            pltpu.VMEM((learn_cols, width), bf16),
+            pltpu.VMEM((dps - 1, learn_cols, learn_rows), bf16),
             pltpu.VMEM((16, width), bf16),
             pltpu.VMEM((dps - 1, 16, width), bf16),
-            dma((2,)), dma((8,)), dma((images,)), dma((dps - 1,)), dma((dps - 1,)),
+            dma(()), dma((7,)), dma((images,)), dma((dps - 1,)), dma((dps - 1,)),
             dma((images,)), dma((images,)), dma((images,)), dma((2, images)), dma((images,)), dma((images,)),
             dma((11, 24)), dma((11, 24)), dma((2, 24)),
             pltpu.SemaphoreType.REGULAR, pltpu.SemaphoreType.REGULAR, dma((2, dps - 1)), dma((2, dps - 1)),
@@ -917,21 +1030,43 @@
             collective_id=0, has_side_effects=True, vmem_limit_bytes=60 * 2**20
         ),
     )(
-        patches, bias, w_query, w_key, w_value, w_out, w_up, w_down,
-        gain_attn[None], gain_mlp[None], gain_learn[None], w_learn, w_select, cotangent,
+        patches.transpose(1, 0, 2).reshape(count * images, width), keep_mask, w_query, w_key, w_value, w_out, w_up, w_down,
+        gain_attn[None], gain_mlp[None], gain_learn[None], w_learn.T, w_select.T, cotangent,
     )
     learned, y, gpat, gall, small, gl = outs
-    y = y.reshape(images, PAD, width)[:, :count]
-    gpat = gpat.reshape(images, PAD, width)[:, :count]
-
-    def stacked(first):
-        v = gall[first : first + 256].reshape(256, 4, 256).astype(f32)
-        return v.transpose(1, 0, 2).reshape(width, 256)
-
+
+    square = (width, TILE)
+    row = (1, width)
+    blocks = -(-count // CH)
+    outs = pl.pallas_call(
+        finish_up,
+        name="finish",
+        out_shape=(
+            sds((images, 8, width), bf16), sds((count, images, width), bf16), sds((count, images, width), bf16),
+            sds(square, f32), sds(square, f32), sds(square, f32),
+            sds((TILE, width), f32), sds((width, hidden), f32), sds((hidden, width), f32),
+            sds(row, f32), sds(row, f32), sds(row, f32),
+            sds((learn_cols, learn_rows), f32), sds((8, learn_cols), f32),
+        ),
+        in_specs=[anywhere] * 3 + [vmem] * 3,
+        out_specs=(vmem,) + (anywhere,) * 8 + (vmem,) * 5,
+        scratch_shapes=[
+            pltpu.VMEM((3072, width), bf16),
+            pltpu.VMEM((images, PAD, width), bf16),
+            pltpu.VMEM((images, PAD, width), bf16),
+            pltpu.VMEM((9 * TILE, width), f32),
+            pltpu.VMEM((3,) + square, f32),
+            pltpu.VMEM((count, images, width), bf16),
+            pltpu.VMEM((count, images, width), bf16),
+            pltpu.VMEM((width // 128, images * CH, 128), f32),
+            dma((12,)), dma((2,)), dma((9,)), dma((3,)), dma((2, blocks)),
+        ],
+        compiler_params=pltpu.CompilerParams(vmem_limit_bytes=60 * 2**20),
+    )(gall, y.reshape(images, PAD, width), gpat.reshape(images, PAD, width), learned, small, gl)
+    learned, y, gpat, gq, gk, gv, gout, gup, gdn, d1, d2, d3, gl, gsel = outs
     return (
-        learned, y, gpat, stacked(2304), stacked(2560), stacked(2816), gall[2048:2304].astype(f32),
-        gall[1024:2048].astype(f32), gall[0:1024].astype(f32),
-        small[0], small[1], small[2], gl, small[8:16, :learn_cols].T,
+        learned, y.transpose(1, 0, 2), gpat.transpose(1, 0, 2), gq, gk, gv, gout, gup, gdn,
+        d1[0], d2[0], d3[0], gl.T, gsel.T,
     )
 
 

time: 291 us -> 259 us (0.89)
  local copies, waits for them, and re-layouts: 28.6 us -> 0 us
  other arithmetic: 10.7 us -> 0 us
  Pallas kernels: 250 us -> 258 us
    unnamed x13 -> x0, local copies, waits for them, and re-layouts: 16.5 us -> none
    pallas_call x0 -> x1, Pallas kernels: none -> 14.1 us  [local_fused(): pl.pallas_call(finish_up, name='finish', out_shape=(sds((images, 8, width...]
    convert_element_type x2 -> x0, other arithmetic: 9.99 us -> none  [the longest x1 6.7 us: local_fused(): gall[0:1024].astype(f32)]
    pallas_call x1, Pallas kernels: 250 us -> 244 us  [local_fused(): pl.pallas_call(fused, name='block', out_shape=(sds((images, 8, width), bf...]
    reshape x6 -> x0, local copies, waits for them, and re-layouts: 6.17 us -> none  [stacked(): return v.transpose(1, 0, 2).reshape(width, 256)]
    slice x3 -> x0, local copies, waits for them, and re-layouts: 4.1 us -> none  [the longest x1 2.27 us: local_fused(): y = y.reshape(images, PAD, width)[:, :count]]
where the time goes in v3:
time: 259 us
  Pallas kernels  258 us (100%)
    pallas_call x1, Pallas kernels, local_fused(): pl.pallas_call(fused, name='block', out_shape=(sds((images, 8, width), bf...  244 us
    pallas_call x1, Pallas kernels, local_fused(): pl.pallas_call(finish_up, name='finish', out_shape=(sds((images, 8, width...  14.1 us

profile of v3, /device:TPU:0, one launch (start us, length us, event | category | flops | bytes accessed | tf_op | source)
XLA Modules:
  0.0 258.8 jit_solution(8617585927819717849)
XLA Ops:
  0.7 243.8 %block.1 = (bf16[8,8,1024]{2,1,0:T(8,128)(2,1)}, bf16[1664,1024]{1,0:T(8,128)(2,1)}, bf16[1664,1024]{1,0:T(8,128)(2,1)}, bf16[3072,1024]{1,0:T(8,128)(2,1)}, f32[16,1024]{1,0:T(8,128)}, /*index=5*/f32[64,128]{1,0:T(8,128)}) custom-call(bf16[1568,1024]{1,0:T(8,128)(2,1)} %bitcast.19, s32[8,196]{1,0:T(8,128)} %keep_ref.1, bf16[1024,256]{1,0:T(8,128)(2,1)} %wq_hbm.1, ...), custom_call_target="tpu_custom_call" | custom-call | tf_op jit(solution)/shard_map/block/pallas_call | solution.py:986
  244.5 14.1 %finish.1 = (bf16[8,8,1024]{2,1,0:T(8,128)(2,1)}, bf16[196,8,1024]{2,1,0:T(8,128)(2,1)}, bf16[196,8,1024]{2,1,0:T(8,128)(2,1)}, f32[1024,256]{1,0:T(8,128)}, f32...) custom-call(bf16[3072,1024]{1,0:T(8,128)(2,1)} %get-tuple-element.34, ...), custom_call_target="tpu_custom_call" | custom-call | tf_op jit(solution)/shard_map/finish/pallas_call | solution.py:1041

commit v4 on v3

--- a/solution.py
+++ b/solution.py
@@ -248,6 +248,7 @@
 TILE = 256
 PAIR_IN = 224
 LAG = 2
+LAG_END = 2
 f32 = jnp.float32
 bf16 = jnp.bfloat16
 
@@ -307,7 +308,7 @@
     learned_ref, y_hbm, gp_hbm, gall_hbm, small_ref, gl_ref,
     bias, wqkv, wo, wl,
     xs, qkv, os, h1s, a2s, dhs, d1s, big, recv,
-    pbuf, rcore, rx, sumb, dg, gl_sum, gsel_sum, gl_mine, gl_in, small_mine, small_in,
+    pbuf, rcore, rx, sumb, dg, gl_sum, gsel_sum, gl_mine, gl_in, small_mine, small_in, col, centre, scale, part_a, part_b,
     sx, sw, sy, slearn_s, slearn_r, s_core, r_core, s_x, r_x, s_ag, r_ag,
     s_pair, r_pair, s_out, ready_y, ready_z, s_small, r_small,
 ):
@@ -354,28 +355,31 @@
         pltpu.make_async_copy(wl_hbm, wl_part(dp), sw.at[6]),
     ]
 
-    load_x = pltpu.make_async_copy(patches, dhs.at[pl.ds(0, images * count)], sx)
-    load_x.start()
-    for k in (0, 1, 2, 3, 6, 4, 5):
+    load_x = [
+        pltpu.make_async_copy(
+            patches.at[:, pl.ds(c * TILE, TILE)], dhs.at[pl.ds(0, images * count), pl.ds(c * TILE, TILE)], sx.at[c]
+        )
+        for c in range(4)
+    ]
+    for copy in load_x:
+        copy.start()
+    for k in (0, 1, 2, 3, 6):
         loads[k].start()
 
-    xs[...] = jnp.zeros_like(xs)
+    for i in range(images):
+        xs[i * PAD + PAD - 16 : (i + 1) * PAD, :] = jnp.zeros((16, width), bf16)
     bias[...] = jnp.full(bias.shape, -1e30, f32)
     for i in range(images):
         bias[i, :, 0:count] = jnp.where(keep_ref[i : i + 1, :] > 0, 0.0, -1e30)
-
-    pl.semaphore_wait(barrier, dps + 1)
-
-    def learn_copy(k):
-        return pltpu.make_async_remote_copy(
-            src_ref=wl_part(dp), dst_ref=wl_part(dp),
-            send_sem=slearn_s.at[k - 1], recv_sem=slearn_r.at[k - 1],
-            device_id=(lax.rem(dp + k, dps), mp), device_id_type=MESH,
-        )
-
-    loads[6].wait()
-    for k in range(1, dps):
-        learn_copy(k).start()
+    turned = jnp.transpose(bias[...].reshape(images, PAD))
+    for i in range(images):
+        col[i * PAD : (i + 1) * PAD, :] = turned[:, i : i + 1]
+    for c in range(4):
+        load_x[c].wait()
+        for r in range(0, images * count, 8 * CH):
+            top = min(r + 8 * CH, images * count)
+            for n in (2 * c, 2 * c + 1):
+                h1s[n, r:top, :] = dhs[r:top, n * 128 : (n + 1) * 128].astype(f32)
 
     g1 = g1_ref[...]
     g2 = g2_ref[...]
@@ -438,14 +442,14 @@
     def store_p(i, t, value):
         pbuf[t // 2, rows_of(i), (t % 2) * TILE : (t % 2 + 1) * TILE] = value.astype(bf16)
 
-    def stage(body, lo, hi, second, before=None):
+    def stage(body, lo, hi, second, before=None, begun=False):
         def step(i, carry):
             if before is not None:
                 before(i, hi)
             body(i)
             copy_core(i).start()
 
-            @pl.when(i > lo)
+            @pl.when((i > lo) | begun)
             def _():
                 second(i - 1)
             return carry
@@ -610,27 +614,34 @@
             z_back(k).wait_recv()
             z_pass(k).wait_recv()
 
-    def tick(t):
-        for h, hop in ((5, hop5), (4, hop4), (3, hop3), (2, hop2), (1, hop1), (0, hop0)):
-            k = t - LAG * h
-
-            @pl.when((k >= 0) & (k < pairs))
+    hops = ((5, hop5), (4, hop4), (3, hop3), (2, hop2), (1, hop1), (0, hop0))
+
+    def tick(t, low, high, lag):
+        for h, hop in hops:
+            k = low + t - lag * h
+
+            @pl.when((k >= low) & (k < high))
             def _(hop=hop, k=k):
                 hop(k)
 
-    def ticks(lo, hi):
+    def tick_mlp(t):
+        tick(t, 0, 16, LAG)
+
+    def tick_attention(t):
+        tick(t, 16, pairs, LAG_END)
+
+    def ticks(run, lo, hi):
         def step(t, carry):
-            tick(t)
+            run(t)
             return carry
 
         lax.fori_loop(lo, hi, step, 0)
 
-    load_x.wait()
-    for r in range(0, images * count, 8 * CH):
-        top = min(r + 8 * CH, images * count)
-        put_wide(pl.ds(r, top - r), dhs[r:top, :].astype(f32))
     for k in (0, 1, 2, 3):
         loads[k].wait()
+    loads[4].start()
+    loads[5].start()
+
 
     def attend(q, k, v, row_bias):
         o = jnp.zeros((PAD, 256), f32)
@@ -661,7 +672,23 @@
         for t in range(4):
             store_p(i, t, nn(ob, wo[:, t * TILE : (t + 1) * TILE]))
 
-    stage(attention_sent, 0, images, far(0))
+    attention_sent(0)
+
+    pl.semaphore_wait(barrier, dps + 1)
+
+    def learn_copy(k):
+        return pltpu.make_async_remote_copy(
+            src_ref=wl_part(dp), dst_ref=wl_part(dp),
+            send_sem=slearn_s.at[k - 1], recv_sem=slearn_r.at[k - 1],
+            device_id=(lax.rem(dp + k, dps), mp), device_id_type=MESH,
+        )
+
+    loads[6].wait()
+    for k in range(1, dps):
+        learn_copy(k).start()
+
+    copy_core(0).start()
+    stage(attention_sent, 1, images, far(0), begun=True)
 
     loads[4].wait()
     loads[5].wait()
@@ -701,8 +728,13 @@
         for r in chunks():
             yb = (get_wide(chunk_of(i, r)) + summed(i, r)).astype(bf16)
             d1s[chunk_of(i, r), :] = yb
-            u, _ = stats(yb.astype(f32))
-            dhs[chunk_of(i, r), :] = (u * g3).astype(bf16)
+            v = yb.astype(f32)
+            mean = jnp.sum(v, axis=-1, keepdims=True) * (1.0 / width)
+            v = v - mean
+            s = lax.rsqrt(jnp.sum(v * v, axis=-1, keepdims=True) * (1.0 / width) + 1e-06)
+            centre[r : r + CH, :] = mean
+            scale[r : r + CH, :] = s
+            dhs[chunk_of(i, r), :] = (v * s * g3).astype(bf16)
         y_out(i).start()
         y = d1s[rows, :]
         a3 = dhs[rows, :]
@@ -713,8 +745,7 @@
         cdf, pdf = gauss(zl)
         t = (zl * cdf).astype(bf16)
         slope = cdf + zl * pdf
-        eye = lax.broadcasted_iota(jnp.int32, (PAD, PAD), 0) == lax.broadcasted_iota(jnp.int32, (PAD, PAD), 1)
-        col_bias = jnp.sum(jnp.where(eye, bias[i], 0.0), axis=1, keepdims=True)
+        col_bias = col[rows, :]
         logits = nt(t, wsel) + col_bias
         e = jnp.exp(logits - jnp.max(logits, axis=0, keepdims=True))
         maps = e * (1.0 / jnp.sum(e, axis=0, keepdims=True))
@@ -725,10 +756,13 @@
         gsel_sum[...] += tn(dlog, t)
         dzl = (nn(dlog, wsel) * slope).astype(bf16)
         gl_sum[...] += tn(dzl, a3)
+        part_a[...] = nn(dzl, wlf)
+        part_b[...] = nn(mb, ct)
         for r in chunks():
-            da3 = nn(dzl[r : r + CH], wlf)
-            dy = nn(mb[r : r + CH], ct)
-            u, s = stats(d1s[chunk_of(i, r), :].astype(f32))
+            da3 = part_a[r : r + CH, :]
+            dy = part_b[r : r + CH, :]
+            s = scale[r : r + CH, :]
+            u = (d1s[chunk_of(i, r), :].astype(f32) - centre[r : r + CH, :]) * s
             dg[2] += fold(da3 * u)
             dhs[chunk_of(i, r), :] = (dy + back(da3 * g3, u, s)).astype(bf16)
 
@@ -743,21 +777,31 @@
         for c in range(4):
             store_p(i, c, nt(dz, wup[c * TILE : (c + 1) * TILE, :]))
 
+    early = images // 2
+
     def learner_mlp(i):
         learner(i)
-        mlp_back(i)
+
+        @pl.when(i < early)
+        def _():
+            mlp_back(i)
+            copy_core(i).start()
+
+        @pl.when((i > 0) & (i <= early))
+        def _():
+            hop_two(i - 1, 0)
 
     hop_three(0, 1)
-    stage(learner_mlp, 0, images, far(0), from_far(1))
-
-    def grad(left, right, first, tick0):
+    each(learner_mlp, 0, images, from_far(1))
+
+    def grad(left, right, first, after):
         def step(j, carry):
             lhs = left[:, pl.ds(pl.multiple_of(j * TILE, TILE), TILE)]
             rows = g_rows(2 * (first + j), 0, TILE)
             for c in range(0, width, TILE):
                 big[rows, c : c + TILE] = tn(lhs, right[:, c : c + TILE]).astype(bf16)
-            if tick0 is not None:
-                tick(tick0 + j)
+            if after is not None:
+                after(j)
             return carry
 
         lax.fori_loop(0, left.shape[1] // TILE, step, 0)
@@ -774,8 +818,22 @@
         pl.semaphore_wait(ready_y, 1)
         pl.semaphore_wait(ready_z, 1)
 
-    grad(rs, dhs, 0, 0)
-    grad(a2s, gs, 4, 4)
+    grad(rs, dhs, 0, tick_mlp)
+
+    def mlp_back_tick(i):
+        mlp_back(i)
+
+        @pl.when(lax.rem(i, 2) == 1)
+        def _():
+            tick_mlp(4 + (i - early) // 2)
+
+    stage(mlp_back_tick, early, images, far(0))
+    def after_up(j):
+        @pl.when(lax.rem(j, 2) == 1)
+        def _():
+            tick_mlp(6 + j // 2)
+
+    grad(a2s, gs, 4, after_up)
     ready()
     for i in range(images):
         y_out(i).wait()
@@ -795,8 +853,7 @@
         q = qkv[rows, 0:256]
         k = qkv[rows, 256:512]
         v = qkv[rows, 512:768]
-        eye = lax.broadcasted_iota(jnp.int32, (PAD, PAD), 0) == lax.broadcasted_iota(jnp.int32, (PAD, PAD), 1)
-        col_bias = jnp.sum(jnp.where(eye, bias[i], 0.0), axis=1, keepdims=True)
+        col_bias = col[rows, :]
         dq = jnp.zeros((PAD, 256), f32)
         dk = jnp.zeros((PAD, 256), f32)
         dv = jnp.zeros((PAD, 256), f32)
@@ -816,12 +873,14 @@
         dall = qkv[rows, :]
         for c in range(4):
             store_p(i, c, nt(dall, wqkv[c * TILE : (c + 1) * TILE, :]))
-        tick(8 + i)
+        tick_mlp(8 + i)
 
     hop_three(0, 0)
     both_ready()
     stage(attention_back, 0, images, far(1), from_far(0))
-    grad(os, d1s, 8, 16)
+    grad(os, d1s, 8, lambda j: tick_mlp(16))
+    tick_attention(0)
+    tick_attention(1)
 
     def grad_qkv(j, carry):
         lhs = a2s[:, pl.ds(pl.multiple_of(j * TILE, TILE), TILE)]
@@ -830,7 +889,8 @@
             rows = pl.ds(pl.multiple_of(1280 + j * 192 + n * 64, 16), 64)
             for c in range(4):
                 big[rows, c * TILE : (c + 1) * TILE] = value[c * 64 : (c + 1) * 64]
-        tick(17 + j)
+        tick_mlp(17 + j)
+        tick_attention(2 + j)
         return carry
 
     lax.fori_loop(0, 4, grad_qkv, 0)
@@ -850,7 +910,8 @@
             dg[0] += fold(da1 * u)
             dhs[where, :] = (d1s[where, :].astype(f32) + back(da1 * g1, u, s)).astype(bf16)
         gp_out(i).start()
-        tick(21 + i)
+        tick_mlp(21 + i)
+        tick_attention(6 + i)
         return carry
 
     hop_three(0, 1)
@@ -883,7 +944,8 @@
     for k in range(1, dps):
         for copy in small_copy(k):
             copy.start()
-    ticks(29, pairs + 5 * LAG)
+    ticks(tick_mlp, 29, 16 + 5 * LAG)
+    ticks(tick_attention, 14, 8 + 5 * LAG_END)
     for k in range(1, dps):
         for copy in small_copy(k):
             copy.wait()
@@ -1021,7 +1083,12 @@
             pltpu.VMEM((dps - 1, learn_cols, learn_rows), bf16),
             pltpu.VMEM((16, width), bf16),
             pltpu.VMEM((dps - 1, 16, width), bf16),
-            dma(()), dma((7,)), dma((images,)), dma((dps - 1,)), dma((dps - 1,)),
+            pltpu.VMEM((total, 1), f32),
+            pltpu.VMEM((PAD, 1), f32),
+            pltpu.VMEM((PAD, 1), f32),
+            pltpu.VMEM((PAD, width), f32),
+            pltpu.VMEM((PAD, width), f32),
+            dma((4,)), dma((7,)), dma((images,)), dma((dps - 1,)), dma((dps - 1,)),
             dma((images,)), dma((images,)), dma((images,)), dma((2, images)), dma((images,)), dma((images,)),
             dma((11, 24)), dma((11, 24)), dma((2, 24)),
             pltpu.SemaphoreType.REGULAR, pltpu.SemaphoreType.REGULAR, dma((2, dps - 1)), dma((2, dps - 1)),

time: 259 us -> 249 us (0.961)
  Pallas kernels: 258 us -> 248 us
    pallas_call x1, Pallas kernels: 244 us -> 234 us  [local_fused(): pl.pallas_call(fused, name='block', out_shape=(sds((images, 8, width), bf...]
where the time goes in v4:
time: 249 us
  Pallas kernels  248 us (100%)
    pallas_call x1, Pallas kernels, local_fused(): pl.pallas_call(fused, name='block', out_shape=(sds((images, 8, width), bf...  234 us
    pallas_call x1, Pallas kernels, local_fused(): pl.pallas_call(finish_up, name='finish', out_shape=(sds((images, 8, width...  14.1 us

profile of v4, /device:TPU:0, one launch (start us, length us, event | category | flops | bytes accessed | tf_op | source)
XLA Modules:
  0.0 248.9 jit_solution(4462418200830544230)
XLA Ops:
  0.7 233.9 %block.1 = (bf16[8,8,1024]{2,1,0:T(8,128)(2,1)}, bf16[1664,1024]{1,0:T(8,128)(2,1)}, bf16[1664,1024]{1,0:T(8,128)(2,1)}, bf16[3072,1024]{1,0:T(8,128)(2,1)}, f32[16,1024]{1,0:T(8,128)}, /*index=5*/f32[64,128]{1,0:T(8,128)}) custom-call(bf16[1568,1024]{1,0:T(8,128)(2,1)} %bitcast.19, s32[8,196]{1,0:T(8,128)} %keep_ref.1, bf16[1024,256]{1,0:T(8,128)(2,1)} %wq_hbm.1, ...), custom_call_target="tpu_custom_call" | custom-call | tf_op jit(solution)/shard_map/block/pallas_call | solution.py:1048
  234.6 14.1 %finish.1 = (bf16[8,8,1024]{2,1,0:T(8,128)(2,1)}, bf16[196,8,1024]{2,1,0:T(8,128)(2,1)}, bf16[196,8,1024]{2,1,0:T(8,128)(2,1)}, f32[1024,256]{1,0:T(8,128)}, f32...) custom-call(bf16[3072,1024]{1,0:T(8,128)(2,1)} %get-tuple-element.34, ...), custom_call_target="tpu_custom_call" | custom-call | tf_op jit(solution)/shard_map/finish/pallas_call | solution.py:1108

commit v5 on v4

--- a/solution.py
+++ b/solution.py
@@ -249,6 +249,8 @@
 PAIR_IN = 224
 LAG = 2
 LAG_END = 2
+QB = 32
+AHEAD = 7
 f32 = jnp.float32
 bf16 = jnp.bfloat16
 
@@ -279,7 +281,7 @@
     mean = jnp.sum(v, axis=-1, keepdims=True) * (1.0 / v.shape[-1])
     c = v - mean
     s = lax.rsqrt(jnp.sum(c * c, axis=-1, keepdims=True) * (1.0 / v.shape[-1]) + 1e-06)
-    return c * s, s
+    return c * s, mean, s
 
 
 def back(e, u, s):
@@ -329,7 +331,6 @@
     mate_e = ((zz + 1 - 2 * lax.rem(zz, 2)) * 2 + yy, mp)
     mate_m = ((3 - zz) * 2 + yy, mp)
     total = images * PAD
-    pairs = 24
     kept = 8 * PAIR_IN
     rs = big.at[pl.ds(0, total)]
     wup = recv.at[pl.ds(kept, width)]
@@ -373,7 +374,7 @@
         bias[i, :, 0:count] = jnp.where(keep_ref[i : i + 1, :] > 0, 0.0, -1e30)
     turned = jnp.transpose(bias[...].reshape(images, PAD))
     for i in range(images):
-        col[i * PAD : (i + 1) * PAD, :] = turned[:, i : i + 1]
+        col[i * PAD : (i + 1) * PAD, 0:1] = turned[:, i : i + 1]
     for c in range(4):
         load_x[c].wait()
         for r in range(0, images * count, 8 * CH):
@@ -477,158 +478,161 @@
 
         lax.fori_loop(lo, hi, step, 0)
 
-    def g_rows(k, lo, n):
-        return pl.ds(pl.multiple_of(lax.rem(k * 128 + 2048, 3072) + lo, 16), n)
-
-    def in_rows(k, lo, n):
-        return pl.ds(pl.multiple_of(k * PAIR_IN + lo, 16), n)
-
-    def send(k, slot, src, dst, device):
-        return pltpu.make_async_remote_copy(
-            src_ref=src, dst_ref=dst, send_sem=s_pair.at[slot, k], recv_sem=r_pair.at[slot, k],
-            device_id=device, device_id_type=MESH,
-        )
-
-    def y_swap(k):
-        return send(k, 0, big.at[g_rows(k, 32 - 32 * yy, 32)], recv.at[in_rows(k, 0, 32)], mate_y)
-
-    def y_end(k):
-        return send(k, 1, big.at[g_rows(k, 32 * yy, 32)], recv.at[in_rows(k, 32, 32)], mate_e)
-
-    def y_mid(k):
-        return send(k, 2, big.at[g_rows(k, 32 * yy, 32)], recv.at[in_rows(k, 64, 32)], mate_m)
-
-    def o_rows(k, lo, n):
-        return gall_hbm.at[pl.ds(pl.multiple_of(k * 128 + lo, 16), n)]
-
-    def y_back(k):
-        return send(k, 3, big.at[g_rows(k, 32 * yy, 32)], o_rows(k, 32 * yy, 32), mate_e)
-
-    def y_share_mid(k):
-        return send(k, 4, big.at[g_rows(k, 32 * yy, 32)], o_rows(k, 32 * yy, 32), mate_y)
-
-    def y_share_end(k):
-        return send(k, 4, o_rows(k, 32 * yy, 32), o_rows(k, 32 * yy, 32), mate_y)
-
-    def z_end(k):
-        return send(k, 5, big.at[g_rows(k, 64, 64)], recv.at[in_rows(k, 160, 64)], mate_e)
-
-    def z_mid(k):
-        return send(k, 6, big.at[g_rows(k, 96 - 32 * zm, 32)], recv.at[in_rows(k, 96, 32)], mate_m)
-
-    def z_swap(k):
-        return send(k, 7, big.at[g_rows(k, 64 + 32 * zm, 32)], recv.at[in_rows(k, 128, 32)], mate_y)
-
-    def z_share(k):
-        return send(k, 8, big.at[g_rows(k, 64 + 32 * zm, 32)], o_rows(k, 64 + 32 * zm, 32), mate_m)
-
-    def z_back(k):
-        return send(k, 9, big.at[g_rows(k, 64 + 32 * zm, 32)], o_rows(k, 64 + 32 * zm, 32), mate_e)
-
-    def z_pass(k):
-        return send(k, 10, o_rows(k, 96 - 32 * zm, 32), o_rows(k, 96 - 32 * zm, 32), mate_e)
-
-    def accumulate(k, lo, n, at):
-        rows = g_rows(k, lo, n)
-        big[rows, :] = (big[rows, :].astype(f32) + recv[in_rows(k, at, n), :].astype(f32)).astype(bf16)
-
-    def keep_y(k):
-        return pltpu.make_async_copy(big.at[g_rows(k, 32 * yy, 32)], o_rows(k, 32 * yy, 32), s_out.at[0, k])
-
-    def keep_z(k):
-        return pltpu.make_async_copy(
-            big.at[g_rows(k, 64 + 32 * zm, 32)], o_rows(k, 64 + 32 * zm, 32), s_out.at[1, k]
-        )
-
-    def hop0(k):
-        y_swap(k).start()
-
-        @pl.when(jnp.logical_not(middle))
-        def _():
-            z_end(k).start()
-
-    def hop1(k):
-        y_swap(k).wait()
-        accumulate(k, 32 * yy, 32, 0)
-
-        @pl.when(middle)
-        def _():
-            z_end(k).wait_recv()
-            accumulate(k, 64, 64, 160)
-            z_mid(k).start()
-
-        @pl.when(jnp.logical_not(middle))
-        def _():
-            y_end(k).start()
-
-    def hop2(k):
-        @pl.when(middle)
-        def _():
-            y_end(k).wait_recv()
-            accumulate(k, 32 * yy, 32, 32)
-            y_mid(k).start()
-            z_mid(k).wait()
-            accumulate(k, 64 + 32 * zm, 32, 96)
-            z_swap(k).start()
-
-    def hop3(k):
-        @pl.when(middle)
-        def _():
-            y_mid(k).wait()
-            accumulate(k, 32 * yy, 32, 64)
-            y_back(k).start()
-            y_share_mid(k).start()
-            keep_y(k).start()
-            z_swap(k).wait()
-            accumulate(k, 64 + 32 * zm, 32, 128)
-            z_share(k).start()
-            z_back(k).start()
-            keep_z(k).start()
-
-    def hop4(k):
-        @pl.when(middle)
-        def _():
-            z_share(k).wait()
-            z_pass(k).start()
-
-        @pl.when(jnp.logical_not(middle))
-        def _():
-            y_end(k).wait_send()
-            y_back(k).wait_recv()
-            y_share_end(k).start()
-
-    def hop5(k):
-        @pl.when(middle)
-        def _():
-            y_share_mid(k).wait()
-            y_back(k).wait_send()
-            z_back(k).wait_send()
-            z_pass(k).wait_send()
-            keep_y(k).wait()
-            keep_z(k).wait()
-
-        @pl.when(jnp.logical_not(middle))
-        def _():
-            y_share_end(k).wait()
-            z_end(k).wait_send()
-            z_back(k).wait_recv()
-            z_pass(k).wait_recv()
-
-    hops = ((5, hop5), (4, hop4), (3, hop3), (2, hop2), (1, hop1), (0, hop0))
-
-    def tick(t, low, high, lag):
-        for h, hop in hops:
-            k = low + t - lag * h
-
-            @pl.when((k >= low) & (k < high))
-            def _(hop=hop, k=k):
-                hop(k)
-
-    def tick_mlp(t):
-        tick(t, 0, 16, LAG)
-
-    def tick_attention(t):
-        tick(t, 16, pairs, LAG_END)
+    def g_tile(j):
+        return pl.ds(pl.multiple_of(lax.rem(j * TILE + 2048, 3072), 16), TILE)
+
+    def pieces(q, count_of, first, number, lag):
+        def g_rows(k, lo, n):
+            return pl.ds(pl.multiple_of(lax.rem(k * (4 * q) + first + 2048, 3072) + lo, 16), n)
+
+        def in_rows(k, lo, n):
+            return pl.ds(pl.multiple_of(k * (7 * q) + first // 128 * PAIR_IN + lo, 16), n)
+
+        def send(k, slot, src, dst, device):
+            return pltpu.make_async_remote_copy(
+                src_ref=src, dst_ref=dst, send_sem=s_pair.at[slot, k + number], recv_sem=r_pair.at[slot, k + number],
+                device_id=device, device_id_type=MESH,
+            )
+
+        def y_swap(k):
+            return send(k, 0, big.at[g_rows(k, q - q * yy, q)], recv.at[in_rows(k, 0, q)], mate_y)
+
+        def y_end(k):
+            return send(k, 1, big.at[g_rows(k, q * yy, q)], recv.at[in_rows(k, q, q)], mate_e)
+
+        def y_mid(k):
+            return send(k, 2, big.at[g_rows(k, q * yy, q)], recv.at[in_rows(k, 2 * q, q)], mate_m)
+
+        def o_rows(k, lo, n):
+            return gall_hbm.at[pl.ds(pl.multiple_of(k * (4 * q) + first + lo, 16), n)]
+
+        def y_back(k):
+            return send(k, 3, big.at[g_rows(k, q * yy, q)], o_rows(k, q * yy, q), mate_e)
+
+        def y_share_mid(k):
+            return send(k, 4, big.at[g_rows(k, q * yy, q)], o_rows(k, q * yy, q), mate_y)
+
+        def y_share_end(k):
+            return send(k, 4, o_rows(k, q * yy, q), o_rows(k, q * yy, q), mate_y)
+
+        def z_end(k):
+            return send(k, 5, big.at[g_rows(k, 2 * q, 2 * q)], recv.at[in_rows(k, 5 * q, 2 * q)], mate_e)
+
+        def z_mid(k):
+            return send(k, 6, big.at[g_rows(k, 3 * q - q * zm, q)], recv.at[in_rows(k, 3 * q, q)], mate_m)
+
+        def z_swap(k):
+            return send(k, 7, big.at[g_rows(k, 2 * q + q * zm, q)], recv.at[in_rows(k, 4 * q, q)], mate_y)
+
+        def z_share(k):
+            return send(k, 8, big.at[g_rows(k, 2 * q + q * zm, q)], o_rows(k, 2 * q + q * zm, q), mate_m)
+
+        def z_back(k):
+            return send(k, 9, big.at[g_rows(k, 2 * q + q * zm, q)], o_rows(k, 2 * q + q * zm, q), mate_e)
+
+        def z_pass(k):
+            return send(k, 10, o_rows(k, 3 * q - q * zm, q), o_rows(k, 3 * q - q * zm, q), mate_e)
+
+        def accumulate(k, lo, n, at):
+            rows = g_rows(k, lo, n)
+            big[rows, :] = (big[rows, :].astype(f32) + recv[in_rows(k, at, n), :].astype(f32)).astype(bf16)
+
+        def keep_y(k):
+            return pltpu.make_async_copy(big.at[g_rows(k, q * yy, q)], o_rows(k, q * yy, q), s_out.at[0, k + number])
+
+        def keep_z(k):
+            return pltpu.make_async_copy(
+                big.at[g_rows(k, 2 * q + q * zm, q)], o_rows(k, 2 * q + q * zm, q), s_out.at[1, k + number]
+            )
+
+        def hop0(k):
+            y_swap(k).start()
+
+            @pl.when(jnp.logical_not(middle))
+            def _():
+                z_end(k).start()
+
+        def hop1(k):
+            y_swap(k).wait()
+            accumulate(k, q * yy, q, 0)
+
+            @pl.when(middle)
+            def _():
+                z_end(k).wait_recv()
+                accumulate(k, 2 * q, 2 * q, 5 * q)
+                z_mid(k).start()
+
+            @pl.when(jnp.logical_not(middle))
+            def _():
+                y_end(k).start()
+
+        def hop2(k):
+            @pl.when(middle)
+            def _():
+                y_end(k).wait_recv()
+                accumulate(k, q * yy, q, q)
+                y_mid(k).start()
+                z_mid(k).wait()
+                accumulate(k, 2 * q + q * zm, q, 3 * q)
+                z_swap(k).start()
+
+        def hop3(k):
+            @pl.when(middle)
+            def _():
+                y_mid(k).wait()
+                accumulate(k, q * yy, q, 2 * q)
+                y_back(k).start()
+                y_share_mid(k).start()
+                keep_y(k).start()
+                z_swap(k).wait()
+                accumulate(k, 2 * q + q * zm, q, 4 * q)
+                z_share(k).start()
+                z_back(k).start()
+                keep_z(k).start()
+
+        def hop4(k):
+            @pl.when(middle)
+            def _():
+                z_share(k).wait()
+                z_pass(k).start()
+
+            @pl.when(jnp.logical_not(middle))
+            def _():
+                y_end(k).wait_send()
+                y_back(k).wait_recv()
+                y_share_end(k).start()
+
+        def hop5(k):
+            @pl.when(middle)
+            def _():
+                y_share_mid(k).wait()
+                y_back(k).wait_send()
+                z_back(k).wait_send()
+                z_pass(k).wait_send()
+                keep_y(k).wait()
+                keep_z(k).wait()
+
+            @pl.when(jnp.logical_not(middle))
+            def _():
+                y_share_end(k).wait()
+                z_end(k).wait_send()
+                z_back(k).wait_recv()
+                z_pass(k).wait_recv()
+
+        hops = ((5, hop5), (4, hop4), (3, hop3), (2, hop2), (1, hop1), (0, hop0))
+
+        def tick(t):
+            for h, hop in hops:
+                k = t - lag * h
+
+                @pl.when((k >= 0) & (k < count_of))
+                def _(hop=hop, k=k):
+                    hop(k)
+
+        return tick
+
+    tick_mlp = pieces(32, 16, 0, 0, LAG)
+    tick_attention = pieces(QB, 256 // QB, 2048, 16, LAG_END)
 
     def ticks(run, lo, hi):
         def step(t, carry):
@@ -657,7 +661,9 @@
         for c in range(width // 128):
             xs[pl.ds(start, count), c * 128 : (c + 1) * 128] = h1s[c, pl.ds(i, count, stride=images), :].astype(bf16)
         for r in chunks():
-            u, _ = stats(xs[chunk_of(i, r), :].astype(f32))
+            u, mean, s = stats(xs[chunk_of(i, r), :].astype(f32))
+            col[chunk_of(i, r), 1:2] = mean
+            col[chunk_of(i, r), 2:3] = s
             a2s[chunk_of(i, r), :] = (u * g1).astype(bf16)
         rows = rows_of(i)
         a1 = a2s[rows, :]
@@ -697,7 +703,9 @@
         for r in chunks():
             h1 = xs[chunk_of(i, r), :].astype(f32) + summed(i, r)
             put_wide(chunk_of(i, r), h1)
-            u, _ = stats(h1)
+            u, mean, s = stats(h1)
+            col[chunk_of(i, r), 3:4] = mean
+            col[chunk_of(i, r), 4:5] = s
             a2s[chunk_of(i, r), :] = (u * g2).astype(bf16)
         rows = rows_of(i)
         a2 = a2s[rows, :]
@@ -745,7 +753,7 @@
         cdf, pdf = gauss(zl)
         t = (zl * cdf).astype(bf16)
         slope = cdf + zl * pdf
-        col_bias = col[rows, :]
+        col_bias = col[rows, 0:1]
         logits = nt(t, wsel) + col_bias
         e = jnp.exp(logits - jnp.max(logits, axis=0, keepdims=True))
         maps = e * (1.0 / jnp.sum(e, axis=0, keepdims=True))
@@ -797,7 +805,7 @@
     def grad(left, right, first, after):
         def step(j, carry):
             lhs = left[:, pl.ds(pl.multiple_of(j * TILE, TILE), TILE)]
-            rows = g_rows(2 * (first + j), 0, TILE)
+            rows = g_tile(first + j)
             for c in range(0, width, TILE):
                 big[rows, c : c + TILE] = tn(lhs, right[:, c : c + TILE]).astype(bf16)
             if after is not None:
@@ -822,17 +830,16 @@
 
     def mlp_back_tick(i):
         mlp_back(i)
-
-        @pl.when(lax.rem(i, 2) == 1)
-        def _():
-            tick_mlp(4 + (i - early) // 2)
+        tick_mlp(4 + i - early)
 
     stage(mlp_back_tick, early, images, far(0))
     def after_up(j):
         @pl.when(lax.rem(j, 2) == 1)
         def _():
-            tick_mlp(6 + j // 2)
-
+            tick_mlp(8 + j // 2)
+
+    ready()
+    both_ready()
     grad(a2s, gs, 4, after_up)
     ready()
     for i in range(images):
@@ -843,17 +850,18 @@
         for r in chunks():
             where = chunk_of(i, r)
             da2 = summed(i, r)
-            u, s = stats(get_wide(where))
+            s = col[where, 4:5]
+            u = (get_wide(where) - col[where, 3:4]) * s
             dg[1] += fold(da2 * u)
             d1s[where, :] = (dhs[where, :].astype(f32) + back(da2 * g2, u, s)).astype(bf16)
-            ux, _ = stats(xs[where, :].astype(f32))
+            ux = (xs[where, :].astype(f32) - col[where, 1:2]) * col[where, 2:3]
             a2s[where, :] = (ux * g1).astype(bf16)
         d1 = d1s[rows, :]
         do = nt(d1, wo[...]).astype(bf16)
         q = qkv[rows, 0:256]
         k = qkv[rows, 256:512]
         v = qkv[rows, 512:768]
-        col_bias = col[rows, :]
+        col_bias = col[rows, 0:1]
         dq = jnp.zeros((PAD, 256), f32)
         dk = jnp.zeros((PAD, 256), f32)
         dv = jnp.zeros((PAD, 256), f32)
@@ -873,12 +881,12 @@
         dall = qkv[rows, :]
         for c in range(4):
             store_p(i, c, nt(dall, wqkv[c * TILE : (c + 1) * TILE, :]))
-        tick_mlp(8 + i)
+        tick_mlp(10 + i)
 
     hop_three(0, 0)
+    stage(attention_back, 0, images, far(1), from_far(0))
     both_ready()
-    stage(attention_back, 0, images, far(1), from_far(0))
-    grad(os, d1s, 8, lambda j: tick_mlp(16))
+    grad(os, d1s, 8, lambda j: tick_mlp(18))
     tick_attention(0)
     tick_attention(1)
 
@@ -889,7 +897,7 @@
             rows = pl.ds(pl.multiple_of(1280 + j * 192 + n * 64, 16), 64)
             for c in range(4):
                 big[rows, c * TILE : (c + 1) * TILE] = value[c * 64 : (c + 1) * 64]
-        tick_mlp(17 + j)
+        tick_mlp(19 + j)
         tick_attention(2 + j)
         return carry
 
@@ -906,11 +914,12 @@
         for r in chunks():
             where = chunk_of(i, r)
             da1 = summed(i, r)
-            u, s = stats(xs[where, :].astype(f32))
+            s = col[where, 2:3]
+            u = (xs[where, :].astype(f32) - col[where, 1:2]) * s
             dg[0] += fold(da1 * u)
             dhs[where, :] = (d1s[where, :].astype(f32) + back(da1 * g1, u, s)).astype(bf16)
         gp_out(i).start()
-        tick_mlp(21 + i)
+        tick_mlp(23 + i)
         tick_attention(6 + i)
         return carry
 
@@ -944,8 +953,8 @@
     for k in range(1, dps):
         for copy in small_copy(k):
             copy.start()
-    ticks(tick_mlp, 29, 16 + 5 * LAG)
-    ticks(tick_attention, 14, 8 + 5 * LAG_END)
+    ticks(tick_mlp, 31, 16 + 5 * LAG)
+    ticks(tick_attention, 14, 16)
     for k in range(1, dps):
         for copy in small_copy(k):
             copy.wait()
@@ -954,6 +963,7 @@
     for k in range(dps - 1):
         small_ref[...] += small_in[k].astype(f32)
         gl_ref[...] += gl_in[k].astype(f32)
+    ticks(tick_attention, 16, 256 // QB + 5 * LAG_END)
     for i in range(images):
         gp_out(i).wait()
 
@@ -971,16 +981,18 @@
         return pltpu.make_async_copy(gall.at[rows], tiles.at[rows], s_tile.at[j])
 
     ins = [pltpu.make_async_copy(y, y_in, s_in.at[0]), pltpu.make_async_copy(gp, gp_in, s_in.at[1])]
-    for j in range(4):
-        tile_in(j).start()
-    for copy in ins:
-        copy.start()
-    for j in range(4, 12):
-        tile_in(j).start()
+    queue = [tile_in(j) for j in range(5)] + ins[:1] + [tile_in(j) for j in range(5, 9)] + ins[1:]
+    queue += [tile_in(j) for j in range(9, 12)]
     outs = []
+
+    def begin(n):
+        for _ in range(n):
+            if queue:
+                queue.pop(0).start()
 
     def tile_out(j):
         tile_in(j).wait()
+        begin(1)
         rows = slice(j * TILE, (j + 1) * TILE)
         wide[rows, :] = tiles[rows, :].astype(f32)
         ref, first = ((gdn_ref, 0), (gup_ref, 4), (gout_ref, 8))[j // 4]
@@ -992,6 +1004,7 @@
 
     def turn(n, src, dst, ref):
         ins[n].wait()
+        begin(2)
         for block in range(0, count, CH):
             rows = min(CH, count - block)
             for c in range(src.shape[2] // 128):
@@ -1006,12 +1019,14 @@
             copy.start()
             outs.append(copy)
 
-    for j in range(4):
+    begin(AHEAD)
+    for j in range(6):
         tile_out(j)
     turn(0, y_in, y_turned, y_ref)
-    for j in range(4, 9):
+    for j in range(6, 9):
         tile_out(j)
     turn(1, gp_in, gp_turned, gp_ref)
+    begin(len(queue))
     for j in range(9, 12):
         tile_in(j).wait()
     for n, ref in enumerate((gq_ref, gk_ref, gv_ref)):
@@ -1083,14 +1098,14 @@
             pltpu.VMEM((dps - 1, learn_cols, learn_rows), bf16),
             pltpu.VMEM((16, width), bf16),
             pltpu.VMEM((dps - 1, 16, width), bf16),
-            pltpu.VMEM((total, 1), f32),
+            pltpu.VMEM((total, 8), f32),
             pltpu.VMEM((PAD, 1), f32),
             pltpu.VMEM((PAD, 1), f32),
             pltpu.VMEM((PAD, width), f32),
             pltpu.VMEM((PAD, width), f32),
             dma((4,)), dma((7,)), dma((images,)), dma((dps - 1,)), dma((dps - 1,)),
             dma((images,)), dma((images,)), dma((images,)), dma((2, images)), dma((images,)), dma((images,)),
-            dma((11, 24)), dma((11, 24)), dma((2, 24)),
+            dma((11, 16 + 256 // QB)), dma((11, 16 + 256 // QB)), dma((2, 16 + 256 // QB)),
             pltpu.SemaphoreType.REGULAR, pltpu.SemaphoreType.REGULAR, dma((2, dps - 1)), dma((2, dps - 1)),
         ],
         compiler_params=pltpu.CompilerParams(

time: 249 us -> 248 us (level)
  no operation moved by 1% of the time
where the time goes in v5:
time: 248 us
  Pallas kernels  247 us (100%)
    pallas_call x1, Pallas kernels, local_fused(): pl.pallas_call(fused, name='block', out_shape=(sds((images, 8, width), bf...  234 us
    pallas_call x1, Pallas kernels, local_fused(): pl.pallas_call(finish_up, name='finish', out_shape=(sds((images, 8, width...  13.7 us

profile of v5, /device:TPU:0, one launch (start us, length us, event | category | flops | bytes accessed | tf_op | source)
XLA Modules:
  0.0 248.1 jit_solution(16095292057094663873)
XLA Ops:
  0.7 233.6 %block.1 = (bf16[8,8,1024]{2,1,0:T(8,128)(2,1)}, bf16[1664,1024]{1,0:T(8,128)(2,1)}, bf16[1664,1024]{1,0:T(8,128)(2,1)}, bf16[3072,1024]{1,0:T(8,128)(2,1)}, f32[16,1024]{1,0:T(8,128)}, /*index=5*/f32[64,128]{1,0:T(8,128)}) custom-call(bf16[1568,1024]{1,0:T(8,128)(2,1)} %bitcast.19, s32[8,196]{1,0:T(8,128)} %keep_ref.1, bf16[1024,256]{1,0:T(8,128)(2,1)} %wq_hbm.1, ...), custom_call_target="tpu_custom_call" | custom-call | tf_op jit(solution)/shard_map/block/pallas_call | solution.py:1063
  234.3 13.7 %finish.1 = (bf16[8,8,1024]{2,1,0:T(8,128)(2,1)}, bf16[196,8,1024]{2,1,0:T(8,128)(2,1)}, bf16[196,8,1024]{2,1,0:T(8,128)(2,1)}, f32[1024,256]{1,0:T(8,128)}, f32...) custom-call(bf16[3072,1024]{1,0:T(8,128)(2,1)} %get-tuple-element.34, ...), custom_call_target="tpu_custom_call" | custom-call | tf_op jit(solution)/shard_map/finish/pallas_call | solution.py:1123

commit v6 on v5

--- a/solution.py
+++ b/solution.py
@@ -694,7 +694,8 @@
         learn_copy(k).start()
 
     copy_core(0).start()
-    stage(attention_sent, 1, images, far(0), begun=True)
+    hop_two(0, 0)
+    stage(attention_sent, 1, images, far(0))
 
     loads[4].wait()
     loads[5].wait()
@@ -799,8 +800,18 @@
         def _():
             hop_two(i - 1, 0)
 
+        @pl.when(i == images - 2)
+        def _():
+            hop_three(i + 1, 1)
+
     hop_three(0, 1)
-    each(learner_mlp, 0, images, from_far(1))
+    def before_learner(i, hi):
+        @pl.when(i + 2 < hi)
+        def _():
+            hop_three(i + 1, 1)
+        arrived(i)
+
+    each(learner_mlp, 0, images, before_learner)
 
     def grad(left, right, first, after):
         def step(j, carry):

time: 248 us -> 246 us (level)
  no operation moved by 1% of the time
where the time goes in v6:
time: 246 us
  Pallas kernels  245 us (100%)
    pallas_call x1, Pallas kernels, local_fused(): pl.pallas_call(fused, name='block', out_shape=(sds((images, 8, width), bf...  232 us
    pallas_call x1, Pallas kernels, local_fused(): pl.pallas_call(finish_up, name='finish', out_shape=(sds((images, 8, width...  13.7 us

profile of v6, /device:TPU:0, one launch (start us, length us, event | category | flops | bytes accessed | tf_op | source)
XLA Modules:
  0.0 246.2 jit_solution(11507430386934013150)
XLA Ops:
  0.7 231.7 %block.1 = (bf16[8,8,1024]{2,1,0:T(8,128)(2,1)}, bf16[1664,1024]{1,0:T(8,128)(2,1)}, bf16[1664,1024]{1,0:T(8,128)(2,1)}, bf16[3072,1024]{1,0:T(8,128)(2,1)}, f32[16,1024]{1,0:T(8,128)}, /*index=5*/f32[64,128]{1,0:T(8,128)}) custom-call(bf16[1568,1024]{1,0:T(8,128)(2,1)} %bitcast.19, s32[8,196]{1,0:T(8,128)} %keep_ref.1, bf16[1024,256]{1,0:T(8,128)(2,1)} %wq_hbm.1, ...), custom_call_target="tpu_custom_call" | custom-call | tf_op jit(solution)/shard_map/block/pallas_call | solution.py:1074
  232.3 13.7 %finish.1 = (bf16[8,8,1024]{2,1,0:T(8,128)(2,1)}, bf16[196,8,1024]{2,1,0:T(8,128)(2,1)}, bf16[196,8,1024]{2,1,0:T(8,128)(2,1)}, f32[1024,256]{1,0:T(8,128)}, f32...) custom-call(bf16[3072,1024]{1,0:T(8,128)(2,1)} %get-tuple-element.34, ...), custom_call_target="tpu_custom_call" | custom-call | tf_op jit(solution)/shard_map/finish/pallas_call | solution.py:1134

commit v7 on v6

--- a/solution.py
+++ b/solution.py
@@ -894,8 +894,18 @@
             store_p(i, c, nt(dall, wqkv[c * TILE : (c + 1) * TILE, :]))
         tick_mlp(10 + i)
 
+        @pl.when(i == images - 2)
+        def _():
+            hop_three(i + 1, 0)
+
     hop_three(0, 0)
-    stage(attention_back, 0, images, far(1), from_far(0))
+    def before_back(i, hi):
+        @pl.when(i + 2 < hi)
+        def _():
+            hop_three(i + 1, 0)
+        arrived(i)
+
+    stage(attention_back, 0, images, far(1), before_back)
     both_ready()
     grad(os, d1s, 8, lambda j: tick_mlp(18))
     tick_attention(0)

time: 246 us -> 246 us (level)
  no operation moved by 1% of the time
where the time goes in v7:
time: 246 us
  Pallas kernels  245 us (100%)
    pallas_call x1, Pallas kernels, local_fused(): pl.pallas_call(fused, name='block', out_shape=(sds((images, 8, width), bf...  232 us
    pallas_call x1, Pallas kernels, local_fused(): pl.pallas_call(finish_up, name='finish', out_shape=(sds((images, 8, width...  13.7 us

profile of v7, /device:TPU:0, one launch (start us, length us, event | category | flops | bytes accessed | tf_op | source)
XLA Modules:
  0.0 246.2 jit_solution(5194435642841969072)
XLA Ops:
  0.7 231.7 %block.1 = (bf16[8,8,1024]{2,1,0:T(8,128)(2,1)}, bf16[1664,1024]{1,0:T(8,128)(2,1)}, bf16[1664,1024]{1,0:T(8,128)(2,1)}, bf16[3072,1024]{1,0:T(8,128)(2,1)}, f32[16,1024]{1,0:T(8,128)}, /*index=5*/f32[64,128]{1,0:T(8,128)}) custom-call(bf16[1568,1024]{1,0:T(8,128)(2,1)} %bitcast.19, s32[8,196]{1,0:T(8,128)} %keep_ref.1, bf16[1024,256]{1,0:T(8,128)(2,1)} %wq_hbm.1, ...), custom_call_target="tpu_custom_call" | custom-call | tf_op jit(solution)/shard_map/block/pallas_call | solution.py:1084
  232.3 13.7 %finish.1 = (bf16[8,8,1024]{2,1,0:T(8,128)(2,1)}, bf16[196,8,1024]{2,1,0:T(8,128)(2,1)}, bf16[196,8,1024]{2,1,0:T(8,128)(2,1)}, f32[1024,256]{1,0:T(8,128)}, f32...) custom-call(bf16[3072,1024]{1,0:T(8,128)(2,1)} %get-tuple-element.34, ...), custom_call_target="tpu_custom_call" | custom-call | tf_op jit(solution)/shard_map/finish/pallas_call | solution.py:1144
